TPU v7x, 32 devices: a whole 2x2x4 slice. The times are simulated.
32 devices in a mesh: groups: 2 (over x), region: 16 (over z, y, core).
Axes of the slice: x: 2, y: 2, z: 4, core: 2. Of those that a mesh axis runs over, the one named last changes fastest.
Arguments:
- successor: int32 [4, 262144], P(None, ('groups', 'region')), parts along dimension 1, may hold values from 0 to 12287, as said below
- send_rows: int32 [32, 16, 256], P(('groups', 'region')), parts along dimension 0, may hold values from 0 to 8191, as said below
- rewards: float32 [4, 262144], P(None, ('groups', 'region')), parts along dimension 1, may hold values from -3 to -0.2
- value_init: float32 [16, 262144], P(None, ('groups', 'region')), parts along dimension 1, may hold values from -6 to 6
- start_mass: float32 [16, 262144], P(None, ('groups', 'region')), parts along dimension 1, may hold values from 0 to 1
- dest: int32 [32], P('groups'), parts along dimension 0, may hold values from 0 to 131071
Outputs:
- values: float32 [16, 262144], P(None, ('groups', 'region')), parts along dimension 1
- edge_visits: float32 [4, 262144], P(None, ('groups', 'region')), parts along dimension 1
- arrival: float32 [16, 262144], P(None, ('groups', 'region')), parts along dimension 1
- log_partition: float32 [32], P('groups'), parts along dimension 0
There are 2 independent parts, one for each index of `groups`. A program takes and returns all parts, laid end to end along the dimension named above; each array names one. Nothing has to cross between parts.
Inputs may be any that keep to these rules, and one draw needn't show every extreme that they name: `successor`: every index below 8192 names an own segment; a boundary slot 8192 + i * 256 + b is named only where b is below the live count of peer i, which is at least 1. `send_rows`: local segment rows; slots past the live count are padding and not read by any edge.
All inputs are finite; a program needn't handle non-finite values.
Results may differ from a plain program's by a relative error of at most 0.00002.
Values sent between devices are 32-bit elements; how exact they have to be, the bound alone decides.
A program may use at most 128 MiB of HBM per device.

v0:
```python
import jax
import jax.numpy as jnp
from jax import lax
from jax.sharding import PartitionSpec as P


def local(successor, send_rows, rewards, value_init, start_mass, dest):
    seg_count = successor.shape[1]
    peers = lax.axis_size("region")
    me_index = lax.axis_index("region")
    slots = send_rows.shape[2]
    own_rows = send_rows[0]
    dest_count = value_init.shape[0]
    positions = lax.broadcasted_iota(jnp.int32, (dest_count, seg_count), 1) + me_index * seg_count
    is_dest = positions == dest[:, None]

    def ghosts(value):
        received = lax.all_to_all(
            value[:, own_rows], "region", split_axis=1, concat_axis=1, tiled=True
        )
        return received.reshape(dest_count, peers * slots)

    def backup(value):
        q_value = rewards[None] + jnp.concatenate([value, ghosts(value)], axis=1)[:, successor]
        new_value = jnp.log(jnp.sum(jnp.exp(q_value), axis=1))
        return (jnp.where(is_dest, jnp.float32(0.0), new_value), q_value)

    first, _ = backup(value_init)
    values, q_value = backup(first)
    policy = jnp.exp(q_value - values[:, None])
    policy = jnp.where(is_dest[:, None], jnp.float32(0.0), policy)

    def spread(mass):
        flow = mass[:, None] * policy
        landed = (
            jnp.zeros((dest_count, seg_count + peers * slots), jnp.float32)
            .at[:, successor]
            .add(flow)
        )
        return (landed, landed[:, seg_count:].reshape(dest_count, peers, slots))

    def settle(landed, inward):
        return landed[:, :seg_count].at[:, own_rows].add(inward)

    weighted = jnp.sum(start_mass * values, axis=1)
    landed, outward = spread(start_mass)
    inward = lax.all_to_all(outward, "region", split_axis=1, concat_axis=1, tiled=True)
    log_partition = lax.psum(weighted, "region")
    mass_one = settle(landed, inward)
    landed, outward = spread(mass_one)
    inward = lax.all_to_all(outward, "region", split_axis=1, concat_axis=1, tiled=True)
    arrival = settle(landed, inward)
    edge_visits = jnp.sum((start_mass + mass_one)[:, None] * policy, axis=0)
    return (values, edge_visits, arrival, log_partition)


def solution(mesh):
    placed = (
        P(None, ("groups", "region")),
        P(("groups", "region"), None, None),
        P(None, ("groups", "region")),
        P(None, ("groups", "region")),
        P(None, ("groups", "region")),
        P("groups"),
    )
    return jax.shard_map(
        local,
        mesh=mesh,
        in_specs=placed,
        out_specs=(
            P(None, ("groups", "region")),
            P(None, ("groups", "region")),
            P(None, ("groups", "region")),
            P("groups"),
        ),
        check_vma=False,
    )
```

profile of v0, /device:TPU:0, one launch (start us, length us, event | category | flops | bytes accessed | tf_op | source)
XLA Modules:
  0.0 847.9 jit_solution(18364916344607563622)
XLA Ops:
  0.6 0.0 copy-start.5
  0.7 0.8 fusion.10
  1.5 3.5 copy.49
  5.0 13.0 %gather_fusion = f32[4096,16]{1,0:T(8,128)S(1)} fusion(f32[16,8192]{0,1:T(8,128)} %copy.49, s32[4096]{0:T(1024)S(1)} %broadcast_clamp_fusion.1), kind=kCustom, calls=%fused_computation | custom fusion | bytes 540672 | tf_op jit(solution)/shard_map/gather | solution.py:19
  17.9 1.3 copy.50
  19.2 7.4 all-to-all-start
  26.7 9.9 %all-to-all-done = f32[16,16,256]{2,0,1:T(8,128)S(1)} async-done(((f32[16,16,256]{2,0,1:T(8,128)}), f32[16,16,256]{2,0,1:T(8,128)S(1)}, u32[]{:S(2)}, u32[]{:S(2)}) %all-to-all-start) | async-done | bytes 262176 | tf_op jit(solution)/shard_map/all_to_all | solution.py:18
  36.7 0.1 pad_maximum_fusion.1
  36.7 4.0 copy.52
  40.7 111.0 %gather_fusion.1 = f32[32768,16]{1,0:T(8,128)} fusion(f32[16,12288]{0,1:T(8,128)} %copy.52, s32[32768]{0:T(1024)S(1)} %broadcast_clamp_fusion), kind=kCustom, calls=%fused_computation.1 | custom fusion | bytes 4325376 | tf_op jit(solution)/shard_map/gather | solution.py:24
  151.7 11.3 %exponential_reduce_fusion = f32[8192,16]{1,0:T(8,128)S(1)} fusion(f32[4,8192,16]{2,1,0:T(8,128)} %bitcast.53, f32[4,8192]{1,0:T(4,128)S(1)} %copy-done.4), kind=kLoop, calls=%fused_computation.13 | loop fusion | flops 917504 | bytes 2752512 | tf_op jit(solution)/shard_map/reduce_sum | solution.py:25
  163.0 0.0 copy-done.7
  163.0 5.0 bitcast_select_fusion
  168.1 13.0 %gather_fusion.2 = f32[4096,16]{1,0:T(8,128)S(1)} fusion(f32[16,8192]{0,1:T(8,128)} %bitcast_select_fusion, s32[4096]{0:T(1024)S(1)} %broadcast_clamp_fusion.1), kind=kCustom, calls=%fused_computation.2 | custom fusion | bytes 540672 | tf_op jit(solution)/shard_map/gather | solution.py:19
  181.1 1.3 copy.53
  182.3 3.5 all-to-all-start.1
  185.9 3.7 broadcast_compare_fusion
  189.6 3.7 copy.60
  193.3 2.6 all-to-all-done.1
  195.9 1.9 copy.67
  197.8 5.4 pad_maximum_fusion
  203.2 111.0 %gather_fusion.3 = f32[32768,16]{1,0:T(8,128)} fusion(f32[16,12288]{0,1:T(8,128)} %pad_maximum_fusion, s32[32768]{0:T(1024)S(1)} %broadcast_clamp_fusion), kind=kCustom, calls=%fused_computation.3 | custom fusion | bytes 4325376 | tf_op jit(solution)/shard_map/gather | solution.py:24
  314.2 13.6 %fusion = f32[16,8192]{0,1:T(8,128)S(1)} fusion(f32[4,8192,16]{2,1,0:T(8,128)} %bitcast.49, f32[4,8192]{1,0:T(4,128)S(1)} %copy-done.4), kind=kLoop, calls=%fused_computation.10 | loop fusion | flops 917504 | bytes 2752512 | tf_op jit(solution)/shard_map/reduce_sum | solution.py:25
  327.8 0.0 slice-start.3
  327.8 3.8 multiply_reduce_fusion.1
  331.6 7.3 fusion.4
  339.0 177.2 %scatter_custom_fusion = f32[16,12288]{0,1:T(8,128)} fusion(s32[32768]{0:T(1024)S(1)} %bitcast.68, f32[32768,16]{1,0:T(8,128)} %bitcast.55, f32[]{:T(128)} %constant.7.clone.1), kind=kCustom, calls=%fused_computation.23 | custom fusion | flops 524288 | bytes 786944 | tf_op jit(solution)/shard_map/scatter-add | solution.py:38
  516.2 3.1 slice.25
  519.2 2.9 copy.57
  522.1 3.7 all-to-all-start.2
  525.8 4.4 slice.24
  530.2 5.6 all-to-all-done.2
  535.8 1.9 copy.68
  537.8 24.5 %scatter_fusion = f32[16,8192]{0,1:T(8,128)} fusion(f32[16,8192]{0,1:T(8,128)} %slice.24, s32[4096]{0:T(1024)S(1)} %bitcast.71, f32[4096,16]{1,0:T(8,128)} %bitcast.60), kind=kCustom, calls=%fused_computation.5 | custom fusion | flops 65536 | bytes 802816 | tf_op jit(solution)/shard_map/scatter-add | solution.py:43
  562.3 6.2 add.60
  568.4 1.3 copy-done.3
  569.7 23.6 %fusion.3 = (f32[16,4,8192]{0,2,1:T(8,128)}, f32[4,8192]{1,0:T(4,128)}) fusion(f32[4,8192]{1,0:T(4,128)S(1)} %copy-done.4, f32[16,8192]{0,1:T(8,128)S(1)} %copy-done.3, f32[16,8192]{0,1:T(8,128)S(1)} %copy-done.2, pred[16,8192]{0,1:T(8,128)(4,1)S(1)} %broadcast_compare_fusion, f32[32768,16]{1,0:T(8,128)} %gather_fusion.3, f32[4,8192,16]{2,1,0:T(8,128)} %bitcast.50, ...), kind=kLoop, calls=%fused_computation.15 | loop fusion | flops 4685824 | bytes 8257536 | tf_op jit(solution)/shard_map/mul | solution.py:34
  593.3 177.3 %scatter_custom_fusion.2 = f32[16,12288]{0,1:T(8,128)} fusion(s32[32768]{0:T(1024)S(1)} %bitcast.69, f32[32768,16]{1,0:T(8,128)} %bitcast.54, f32[]{:T(128)} %constant.7.clone.1), kind=kCustom, calls=%fused_computation.21 | custom fusion | flops 524288 | bytes 786944 | tf_op jit(solution)/shard_map/scatter-add | solution.py:38
  770.6 1.7 slice.27
  772.4 1.3 copy.61
  773.6 3.5 all-to-all-start.3
  777.2 34.3 %psum.7 = f32[16]{0:T(128)} all-reduce(f32[16]{0:T(128)S(1)} %get-tuple-element.20), channel_id=1, replica_groups=mesh['groups'=2,'region'=16] {'region'}, use_global_device_ids=true, to_apply=%region_8.9 | all-reduce | flops 16 | bytes 128 | tf_op jit(solution)/shard_map/psum | solution.py:48
  811.5 3.5 copy.65
  815.0 4.5 slice.26
  819.5 0.0 all-to-all-done.3
  819.5 0.6 copy.69
  820.1 24.3 %scatter_fusion.1 = f32[16,8192]{0,1:T(8,128)} fusion(f32[16,8192]{0,1:T(8,128)} %slice.26, s32[4096]{0:T(1024)S(1)} %bitcast.72, f32[4096,16]{1,0:T(8,128)S(1)} %bitcast.59), kind=kCustom, calls=%fused_computation.7 | custom fusion | flops 65536 | bytes 802816 | tf_op jit(solution)/shard_map/scatter-add | solution.py:43
  844.4 3.5 copy.66
  (28 shorter events, 0.1 us)
Async XLA Ops:
  0.6 36.0 %copy-start.5 = (f32[16,8192]{1,0:T(8,128)S(1)}, f32[16,8192]{1,0:T(8,128)}, u32[]{:S(2)}) copy-start(f32[16,8192]{1,0:T(8,128)} %param.9) | copy-start | bytes 1572868
  0.6 26.0 %copy-start.6 = (s32[4,8192]{1,0:T(4,128)S(1)}, s32[4,8192]{1,0:T(4,128)}, u32[]{:S(2)}) copy-start(s32[4,8192]{1,0:T(4,128)} %param.6) | copy-start | bytes 393220
  19.2 17.4 %all-to-all-start = ((f32[16,16,256]{2,0,1:T(8,128)}), f32[16,16,256]{2,0,1:T(8,128)S(1)}, u32[]{:S(2)}, u32[]{:S(2)}) async-start(f32[16,16,256]{2,0,1:T(8,128)} %bitcast.2), calls=%async_computation | async-start | bytes 524288 | tf_op jit(solution)/shard_map/all_to_all | solution.py:18
  40.7 111.0 %copy-start.4 = (f32[4,8192]{1,0:T(4,128)S(1)}, f32[4,8192]{1,0:T(4,128)}, u32[]{:S(2)}) copy-start(f32[4,8192]{1,0:T(4,128)} %param.8) | copy-start | bytes 393220
  151.7 11.3 %copy-start.7 = (s32[16]{0:T(128)S(1)}, s32[16]{0:T(128)}, u32[]{:S(2)}) copy-start(s32[16]{0:T(128)} %param.11) | copy-start | bytes 196
  182.3 13.5 %all-to-all-start.1 = ((f32[16,16,256]{2,0,1:T(8,128)}), f32[16,16,256]{2,0,1:T(8,128)S(1)}, u32[]{:S(2)}, u32[]{:S(2)}) async-start(f32[16,16,256]{2,0,1:T(8,128)} %bitcast.6), calls=%async_computation.1 | async-start | bytes 524288 | tf_op jit(solution)/shard_map/all_to_all | solution.py:18
  314.2 13.6 %copy-start = (f32[16,8192]{0,1:T(8,128)S(1)}, f32[16,8192]{0,1:T(8,128)}, u32[]{:S(2)}) copy-start(f32[16,8192]{0,1:T(8,128)} %copy.60) | copy-start | bytes 1572868
  314.2 17.4 %slice-start = ((s8[16777216]{0:T(1024)(128)(4,1)}), s8[4194304]{0:T(1024)(128)(4,1)S(1)}, s32[]{:S(2)}) async-start(s8[16777216]{0:T(1024)(128)(4,1)} %bitcast.51), calls=%async_computation.4 | async-start | bytes 8388608
  314.2 17.4 %slice-start.1 = ((s8[16777216]{0:T(1024)(128)(4,1)}), s8[4194304]{0:T(1024)(128)(4,1)S(1)}, s32[]{:S(2)}) async-start(s8[16777216]{0:T(1024)(128)(4,1)} %bitcast.51), calls=%async_computation.5 | async-start | bytes 8388608
  314.2 17.4 %slice-start.2 = ((s8[16777216]{0:T(1024)(128)(4,1)}), s8[4194304]{0:T(1024)(128)(4,1)S(1)}, s32[]{:S(2)}) async-start(s8[16777216]{0:T(1024)(128)(4,1)} %bitcast.51), calls=%async_computation.6 | async-start | bytes 8388608
  327.8 3.8 slice-start.3
  331.5 7.4 copy-start.1
  522.1 13.7 %all-to-all-start.2 = ((f32[16,16,256]{2,0,1:T(8,128)}), f32[16,16,256]{2,0,1:T(8,128)S(1)}, u32[]{:S(2)}, u32[]{:S(2)}) async-start(f32[16,16,256]{2,0,1:T(8,128)} %copy.57), calls=%async_computation.2 | async-start | bytes 524288 | tf_op jit(solution)/shard_map/all_to_all | solution.py:47
  562.3 6.2 copy-start.2
  562.3 7.4 copy-start.3
  773.6 45.9 %all-to-all-start.3 = ((f32[16,16,256]{2,0,1:T(8,128)}), f32[16,16,256]{2,0,1:T(8,128)S(1)}, u32[]{:S(2)}, u32[]{:S(2)}) async-start(f32[16,16,256]{2,0,1:T(8,128)} %copy.61), calls=%async_computation.3 | async-start | bytes 524288 | tf_op jit(solution)/shard_map/all_to_all | solution.py:51
where the time goes:
time: 849 us; the launch traced here: 848 us
  other arithmetic  484 us (57%)
  local copies, waits for them, and re-layouts  292 us (34%)
  blocking collectives  34.3 us (4%)
  starting transfers between devices  18.2 us (2%)
  waiting for transfers between devices  18.2 us (2%)
    scatter-add x2, other arithmetic, spread(): landed = jnp.zeros((dest_count, seg_count + peers * slots), jnp.float32)....  354 us
    gather x2, local copies, waits for them, and re-layouts, backup(): jnp.concatenate([value, ghosts(value)], axis=1)[:, successor]  222 us
    scatter-add x2, other arithmetic, settle(): return landed[:, :seg_count].at[:, own_rows].add(inward)  48.8 us
    psum x1, blocking collectives, local(): log_partition = lax.psum(weighted, 'region')  34.3 us
    mul x2, other arithmetic, spread(): flow = mass[:, None] * policy  31 us
    gather x4, local copies, waits for them, and re-layouts, ghosts(): value[:, own_rows]  28.5 us
    reduce_sum x2, other arithmetic, backup(): new_value = jnp.log(jnp.sum(jnp.exp(q_value), axis=1))  24.9 us
  transfers between devices with their start and end apart: 4, of which 3 were waited for; matrix products, arithmetic and copies ran while one was open for 2% of the time, Pallas kernels for 0%

commit v1 on v0

v1 whole, which is shorter than its diff:
```python
import functools

import jax
import jax.numpy as jnp
from jax import lax
from jax.experimental import pallas as pl
from jax.experimental.pallas import tpu as pltpu
from jax.sharding import PartitionSpec as P

LANES = 128
VMEM = pl.BlockSpec(memory_space=pltpu.VMEM)
SMEM = pl.BlockSpec(memory_space=pltpu.SMEM)
TABLES = 2


def group_of(rows, dests):
    return lax.broadcasted_iota(jnp.int32, (rows, LANES), 1) // dests


def fold(x, dests):
    shift = dests
    while shift < LANES:
        x = x + pltpu.roll(x, shift, axis=1)
        shift *= 2
    return x


def rows_of(block):
    return jnp.concatenate([block] * (LANES // block.shape[0]), axis=0).T


def ds(start, size):
    return pl.ds(pl.multiple_of(start, size), size)


def pack_send(table, send_rows, out, dests):
    _, peers, slots = send_rows.shape
    groups = LANES // dests
    per = slots // groups
    where = group_of(1, dests)

    @pl.loop(0, peers)
    def _(i):
        @pl.loop(0, per, unroll=4)
        def _(r):
            row = table[pl.ds(send_rows[0, i, r], 1), :]
            for c in range(1, groups):
                other = table[pl.ds(send_rows[0, i, c * per + r], 1), :]
                row = jnp.where(where == c, other, row)
            out[pl.ds(i * per + r, 1), :] = row


def fill(table, own, received, peers, slots, dests):
    seg = own.shape[0]
    groups = LANES // dests
    per = slots // groups
    where = group_of(per, dests)

    @pl.loop(0, seg // 64, unroll=2)
    def _(b):
        table[ds(b * 64, 64), :] = own[ds(b * 64, 64), :]

    @pl.loop(0, peers)
    def _(i):
        block = received[ds(i * per, per), :]
        for c in range(groups):
            one = fold(jnp.where(where == c, block, 0.0), dests)
            table[ds(seg + i * slots + c * per, per), :] = one


def gather(table, successor, out, dests):
    edges, seg = successor.shape
    half = seg // 2
    where = group_of(1, dests)

    @pl.loop(0, half, unroll=4)
    def _(r):
        row = None
        for c in range(2 * edges):
            other = table[pl.ds(successor[c % edges, r + (c // edges) * half], 1), :]
            row = other if row is None else jnp.where(where == c, other, row)
        out[pl.ds(r, 1), :] = row


def scatter(tables, flow, successor, dests):
    edges, seg = successor.shape
    half = seg // 2
    step = half // len(tables)
    where = group_of(1, dests)

    for table in tables:
        @pl.loop(0, table.shape[0] // 64)
        def _(b):
            table[ds(b * 64, 64), :] = jnp.zeros((64, LANES), jnp.float32)

    @pl.loop(0, step, unroll=2)
    def _(r0):
        work = []
        for n, table in enumerate(tables):
            r = r0 + n * step
            row = flow[pl.ds(r, 1), :]
            for c in range(2 * edges):
                at = table.at[pl.ds(successor[c % edges, r + (c // edges) * half], 1), :]
                work.append((at, at[...] + row, where == c))
        for at, value, mask in work:
            pltpu.store(at, value, mask=mask)


def settle(table, received, send_rows, dests):
    _, peers, slots = send_rows.shape
    groups = LANES // dests
    per = slots // groups
    where = group_of(1, dests)

    @pl.loop(0, peers)
    def _(i):
        @pl.loop(0, per, unroll=2)
        def _(r):
            row = received[pl.ds(i * per + r, 1), :]
            work = []
            for c in range(groups):
                at = table.at[pl.ds(send_rows[0, i, c * per + r], 1), :]
                work.append((at, at[...] + row, where == c))
            for at, value, mask in work:
                pltpu.store(at, value, mask=mask)


def total(tables, rows):
    x = tables[0][rows, :]
    for table in tables[1:]:
        x = x + table[rows, :]
    return x


def finish_spread(tables, seg, peers, slots, own_out, send_out, dests):
    groups = LANES // dests
    per = slots // groups
    where = group_of(per, dests)

    @pl.loop(0, seg // 64)
    def _(b):
        own_out[ds(b * 64, 64), :] = total(tables, ds(b * 64, 64))

    @pl.loop(0, peers)
    def _(i):
        block = None
        for c in range(groups):
            one = fold(total(tables, ds(seg + i * slots + c * per, per)), dests)
            block = one if block is None else jnp.where(where == c, one, block)
        send_out[i, pl.ds(0, per), :] = block


def start_kernel(value, send_rows, table, send):
    dests, seg = value.shape

    @pl.loop(0, seg // LANES, unroll=2)
    def _(b):
        table[ds(b * LANES, LANES), :] = rows_of(jnp.exp(value[:, ds(b * LANES, LANES)]))

    pack_send(table, send_rows, send, dests)


def first_kernel(own, received, successor, rewards, dest_at, send_rows, new, weight, send, table, got):
    edges, seg = successor.shape
    _, peers, slots = send_rows.shape
    half = seg // 2
    dests = LANES // (2 * edges)
    fill(table, own, received, peers, slots, dests)
    gather(table, successor, got, dests)
    lane = lax.broadcasted_iota(jnp.int32, (LANES, LANES), 1)
    line = lax.broadcasted_iota(jnp.int32, (LANES, LANES), 0)

    @pl.loop(0, half // LANES)
    def _(b):
        at = ds(b * LANES, LANES)
        both = [jnp.exp(rewards[:, ds(h * half + b * LANES, LANES)]) for h in range(2)]
        lines = [jnp.broadcast_to(x[e : e + 1, :], (dests, LANES)) for x in both for e in range(edges)]
        w = jnp.concatenate(lines, axis=0).T
        weight[at, :] = w
        p = got[at, :] * w
        for h in range(2):
            mine = (lane >= LANES // 2) == (h == 1)
            x = fold(jnp.where(mine, p, 0.0), dests)
            is_dest = line + (h * half + b * LANES) == dest_at[...]
            new[ds(h * half + b * LANES, LANES), :] = jnp.where(is_dest, 1.0, x)

    pack_send(new, send_rows, send, dests)


def second_kernel(own, received, successor, weight, dest_at, start_mass, peers, slots,
                  values, p_out, inverse, landed, send, table, flow, *more):
    edges, seg = successor.shape
    half = seg // 2
    dests = LANES // (2 * edges)
    fill(table, own, received, peers, slots, dests)
    gather(table, successor, p_out, dests)
    lane = lax.broadcasted_iota(jnp.int32, (LANES, LANES), 1)
    line = lax.broadcasted_iota(jnp.int32, (LANES, LANES), 0)

    def body(b, weighted):
        at = ds(b * LANES, LANES)
        w = weight[at, :]
        p = p_out[at, :] * w
        p_out[at, :] = p
        parts = []
        for h in range(2):
            here = ds(h * half + b * LANES, LANES)
            mine = (lane >= LANES // 2) == (h == 1)
            x = fold(jnp.where(mine, p, 0.0), dests)
            is_dest = line + (h * half + b * LANES) == dest_at[...]
            v = jnp.where(is_dest, 0.0, jnp.log(x)).T[:dests, :]
            values[:, here] = v
            mass = start_mass[:, here]
            weighted = weighted + mass * v
            inv = jnp.where(is_dest, 0.0, 1.0 / x)
            inverse[here, :] = inv
            parts.append(rows_of(mass) * inv)
        flow[at, :] = jnp.where(lane >= LANES // 2, parts[1], parts[0]) * w
        return weighted

    weighted = lax.fori_loop(0, half // LANES, body, jnp.zeros((dests, LANES), jnp.float32))
    tables = (table,) + more
    scatter(tables, flow, successor, dests)
    finish_spread(tables, seg, peers, slots, landed, send, dests)
    per = slots * dests // LANES

    @pl.loop(0, peers)
    def _(i):
        send[i, pl.ds(per, dests), :] = weighted


def third_kernel(own, received, successor, weight, start_mass, p_in, inverse, landed_in, send_rows,
                 edge_visits, landed, send, total_out, table, flow, inward, *more):
    edges, seg = successor.shape
    _, peers, slots = send_rows.shape
    half = seg // 2
    dests = LANES // (2 * edges)
    per = slots * dests // LANES
    lane = lax.broadcasted_iota(jnp.int32, (LANES, LANES), 1)

    weighted = jnp.zeros((dests, LANES), jnp.float32)
    for i in range(peers):
        inward[pl.ds(i * per, per), :] = received[i, :per, :]
        weighted = weighted + received[i, per:, :]
    total_out[...] = jnp.broadcast_to(jnp.sum(weighted, axis=1, keepdims=True), (dests, LANES))

    @pl.loop(0, seg // 64)
    def _(b):
        table[ds(b * 64, 64), :] = landed_in[ds(b * 64, 64), :]

    settle(table, inward, send_rows, dests)

    @pl.loop(0, half // LANES)
    def _(b):
        at = ds(b * LANES, LANES)
        visits, parts = [], []
        for h in range(2):
            here = ds(h * half + b * LANES, LANES)
            mass = own[here, :] * fold(table[here, :], dests)
            inv = inverse[here, :]
            parts.append(mass * inv)
            visits.append((rows_of(start_mass[:, here]) + mass) * inv)
        flow[at, :] = jnp.where(lane >= LANES // 2, parts[1], parts[0]) * weight[at, :]
        seen = jnp.where(lane >= LANES // 2, visits[1], visits[0]) * p_in[at, :]
        seen = seen.T
        lines = [jnp.sum(seen[c * dests : (c + 1) * dests, :], axis=0, keepdims=True) for c in range(2 * edges)]
        for h in range(2):
            edge_visits[:, ds(h * half + b * LANES, LANES)] = jnp.concatenate(
                lines[h * edges : (h + 1) * edges], axis=0
            )

    tables = (table,) + more
    scatter(tables, flow, successor, dests)
    finish_spread(tables, seg, peers, slots, landed, send, dests)


def last_kernel(own, received, landed_in, send_rows, arrival, table):
    dests, seg = arrival.shape

    @pl.loop(0, seg // 64)
    def _(b):
        table[ds(b * 64, 64), :] = landed_in[ds(b * 64, 64), :]

    settle(table, received, send_rows, dests)

    @pl.loop(0, seg // LANES)
    def _(b):
        at = ds(b * LANES, LANES)
        arrival[:, at] = (own[at, :] * fold(table[at, :], dests)).T[:dests, :]


def call(kernel, specs, shapes, scratch, name):
    return pl.pallas_call(
        kernel,
        in_specs=specs,
        out_specs=[VMEM] * len(shapes),
        out_shape=[jax.ShapeDtypeStruct(s, jnp.float32) for s in shapes],
        scratch_shapes=[pltpu.VMEM(s, jnp.float32) for s in scratch],
        compiler_params=pltpu.CompilerParams(vmem_limit_bytes=56 * 1024 * 1024),
        name=name,
    )


def local(successor, send_rows, rewards, value_init, start_mass, dest):
    edges, seg = successor.shape
    _, peers, slots = send_rows.shape
    dests = value_init.shape[0]
    half = seg // 2
    groups = LANES // dests
    per = slots // groups
    all_rows = seg + peers * slots
    dest_at = jnp.tile(dest - lax.axis_index("region") * seg, groups)[None]
    rows, packed, sent = (seg, LANES), (half, LANES), (peers * per, LANES)
    big = (all_rows, LANES)
    more = [big] * (TABLES - 1)

    def exchange(x):
        y = lax.all_to_all(
            x.reshape(peers, -1, LANES), "region", split_axis=0, concat_axis=0, tiled=True
        )
        return y.reshape(x.shape)

    zero, send = call(start_kernel, [VMEM, SMEM], [rows, sent], [], "start")(value_init, send_rows)
    one, weight, send = call(
        first_kernel, [VMEM, VMEM, SMEM, VMEM, VMEM, SMEM], [rows, packed, sent], [big, packed], "first"
    )(zero, exchange(send), successor, rewards, dest_at, send_rows)

    def second(own, received, succ, w, d, mass, *rest):
        second_kernel(own, received, succ, w, d, mass, peers, slots, *rest)

    values, p, inverse, landed, send = call(
        second, [VMEM, VMEM, SMEM, VMEM, VMEM, VMEM],
        [(dests, seg), packed, rows, rows, (peers, per + dests, LANES)], [big, packed] + more, "second",
    )(one, exchange(send), successor, weight, dest_at, start_mass)
    edge_visits, landed, send, totals = call(
        third_kernel, [VMEM, VMEM, SMEM, VMEM, VMEM, VMEM, VMEM, VMEM, SMEM],
        [(edges, seg), rows, (peers, per, LANES), (dests, LANES)], [big, packed, sent] + more, "third",
    )(one, exchange(send), successor, weight, start_mass, p, inverse, landed, send_rows)
    (arrival,) = call(last_kernel, [VMEM, VMEM, VMEM, SMEM], [(dests, seg)], [rows], "last")(
        one, exchange(send).reshape(sent), landed, send_rows
    )
    return values, edge_visits, arrival, totals[:, 0]


def solution(mesh):
    placed = (
        P(None, ("groups", "region")),
        P(("groups", "region"), None, None),
        P(None, ("groups", "region")),
        P(None, ("groups", "region")),
        P(None, ("groups", "region")),
        P("groups"),
    )
    return jax.shard_map(
        local,
        mesh=mesh,
        in_specs=placed,
        out_specs=(
            P(None, ("groups", "region")),
            P(None, ("groups", "region")),
            P(None, ("groups", "region")),
            P("groups"),
        ),
        check_vma=False,
    )
```

time: 849 us -> 407 us (0.48)
  other arithmetic: 484 us -> 0.66 us
  Pallas kernels: 0 us -> 343 us
  local copies, waits for them, and re-layouts: 292 us -> 3.35 us
    scatter-add x4 -> x0, other arithmetic: 403 us -> none  [the longest x2 354 us: spread(): landed = jnp.zeros((dest_count, seg_count + peers * slots), jnp.float32)....]
    pallas_call x0 -> x5, Pallas kernels: none -> 343 us  [the longest x1 125 us: local(): call(second, [VMEM, VMEM, SMEM, VMEM, VMEM, VMEM], [(dests, seg), packed,...]
    gather x6 -> x0, local copies, waits for them, and re-layouts: 250 us -> none  [the longest x2 222 us: backup(): jnp.concatenate([value, ghosts(value)], axis=1)[:, successor]]
    psum x1 -> x0, blocking collectives: 34.3 us -> none  [local(): log_partition = lax.psum(weighted, 'region')]
    mul x2 -> x0, other arithmetic: 31 us -> none  [spread(): flow = mass[:, None] * policy]
    all_to_all x0 -> x2, blocking collectives: none -> 30.6 us  [exchange(): lax.all_to_all(x.reshape(peers, -1, LANES), 'region', split_axis=0, conca...]
    reduce_sum x3 -> x0, other arithmetic: 28.6 us -> none  [the longest x2 24.9 us: backup(): new_value = jnp.log(jnp.sum(jnp.exp(q_value), axis=1))]
    unnamed x30 -> x4, local copies, waits for them, and re-layouts: 15.5 us -> 1.43 us
  transfers between devices with their start and end apart: 4 -> 2, of which waited for: 3 -> 2; matrix products, arithmetic and copies ran while one was open for 2% -> 1% of each run, Pallas kernels for 0% -> 0%
where the time goes in v1:
time: 407 us; the launch traced here: 406 us
  Pallas kernels  343 us (84%)
  blocking collectives  30.6 us (8%)
  waiting for transfers between devices  17.5 us (4%)
  starting transfers between devices  10.9 us (3%)
    pallas_call x1, Pallas kernels, local(): call(second, [VMEM, VMEM, SMEM, VMEM, VMEM, VMEM], [(dests, seg), packed,...  125 us
    pallas_call x1, Pallas kernels, local(): call(third_kernel, [VMEM, VMEM, SMEM, VMEM, VMEM, VMEM, VMEM, VMEM, SMEM]...  88.1 us
    pallas_call x1, Pallas kernels, local(): call(first_kernel, [VMEM, VMEM, SMEM, VMEM, VMEM, SMEM], [rows, packed, s...  77.7 us
    pallas_call x1, Pallas kernels, local(): call(last_kernel, [VMEM, VMEM, VMEM, SMEM], [(dests, seg)], [rows], 'last')  34.9 us
    all_to_all x2, blocking collectives, exchange(): lax.all_to_all(x.reshape(peers, -1, LANES), 'region', split_axis=0, conca...  30.6 us
    all_to_all x2, waiting for transfers between devices, exchange(): lax.all_to_all(x.reshape(peers, -1, LANES), 'region', split_axis=0, conca...  17.5 us
    pallas_call x1, Pallas kernels, local(): call(start_kernel, [VMEM, SMEM], [rows, sent], [], 'start')  17.2 us
    all_to_all x2, starting transfers between devices, exchange(): lax.all_to_all(x.reshape(peers, -1, LANES), 'region', split_axis=0, conca...  10.9 us
  transfers between devices with their start and end apart: 2, of which 2 were waited for; matrix products, arithmetic and copies ran while one was open for 1% of the time, Pallas kernels for 0%

profile of v1, /device:TPU:0, one launch (start us, length us, event | category | flops | bytes accessed | tf_op | source)
XLA Modules:
  0.0 406.3 jit_solution(18371033254995416389)
XLA Ops:
  0.6 17.2 %start.1 = (f32[8192,128]{1,0:T(8,128)}, f32[512,128]{1,0:T(8,128)}) custom-call(f32[16,8192]{1,0:T(8,128)} %value.1, s32[1,16,256]{2,1,0:T(8,128)} %send_rows.7), custom_call_target="tpu_custom_call" | custom-call | tf_op jit(solution)/shard_map/start/pallas_call | solution.py:323
  17.9 7.4 %all-to-all-start = ((f32[16,32,128]{2,1,0:T(8,128)}), f32[16,32,128]{2,1,0:T(8,128)S(1)}, u32[]{:S(2)}, u32[]{:S(2)}) async-start(f32[16,32,128]{2,1,0:T(8,128)} %bitcast.8), calls=%async_computation | async-start | bytes 524288 | tf_op jit(solution)/shard_map/all_to_all | solution.py:318
  25.3 0.7 broadcast_subtract_fusion
  25.9 0.6 broadcast_in_dim_tile.3.dest_at.d
  26.5 8.8 %all-to-all-done = f32[16,32,128]{2,1,0:T(8,128)S(1)} async-done(((f32[16,32,128]{2,1,0:T(8,128)}), f32[16,32,128]{2,1,0:T(8,128)S(1)}, u32[]{:S(2)}, u32[]{:S(2)}) %all-to-all-start) | async-done | bytes 262176 | tf_op jit(solution)/shard_map/all_to_all | solution.py:318
  35.3 0.0 copy-start
  35.3 0.7 copy-done
  36.0 77.7 %first.1 = (f32[8192,128]{1,0:T(8,128)}, f32[4096,128]{1,0:T(8,128)}, f32[512,128]{1,0:T(8,128)}) custom-call(f32[8192,128]{1,0:T(8,128)} %get-tuple-element.18.own, f32[512,128]{1,0:T(8,128)} %bitcast.6, s32[4,8192]{1,0:T(4,128)} %successor.3, f32[4,8192]{1,0:T(4,128)} %rewards.1, s32[1,128]{1,0:T(1,128)} %broadcast_in_dim_tile.3.dest_at.d, ...), custom_call_target="tpu_custom_call" | custom-call | tf_op jit(solution)/shard_map/first/pallas_call | solution.py:324
  113.7 14.2 %all_to_all.20 = f32[16,32,128]{2,1,0:T(8,128)} all-to-all(f32[16,32,128]{2,1,0:T(8,128)} %bitcast.9), channel_id=1, replica_groups=mesh['groups'=2,'region'=16] {'region'}, dimensions={0} | all-to-all | bytes 524288 | tf_op jit(solution)/shard_map/all_to_all | solution.py:318
  127.9 124.6 %second.1 = (f32[16,8192]{1,0:T(8,128)}, f32[4096,128]{1,0:T(8,128)}, f32[8192,128]{1,0:T(8,128)}, f32[8192,128]{1,0:T(8,128)}, f32[16,48,128]{2,1,0:T(8,128)}) custom-call(f32[8192,128]{1,0:T(8,128)} %get-tuple-element.20.own, f32[512,128]{1,0:T(8,128)} %bitcast.5, s32[4,8192]{1,0:T(4,128)} %successor.3, f32[4096,128]{1,0:T(8,128)} %get-tuple-element.22.w.weight, ...), custom_call_target="tpu_custom_call" | custom-call | tf_op jit(solution)/shard_map/second/pallas_call | solution.py:331
  252.6 16.4 %all_to_all.21.received = f32[16,48,128]{2,1,0:T(8,128)} all-to-all(f32[16,48,128]{2,1,0:T(8,128)} %get-tuple-element.24), channel_id=1, replica_groups=mesh['groups'=2,'region'=16] {'region'}, dimensions={0} | all-to-all | bytes 786432 | tf_op jit(solution)/shard_map/all_to_all | solution.py:318
  269.0 88.1 %third.1 = (f32[4,8192]{1,0:T(4,128)}, f32[8192,128]{1,0:T(8,128)}, f32[16,32,128]{2,1,0:T(8,128)}, f32[16,128]{1,0:T(8,128)}) custom-call(f32[8192,128]{1,0:T(8,128)} %get-tuple-element.20.own, f32[16,48,128]{2,1,0:T(8,128)} %all_to_all.21.received, s32[4,8192]{1,0:T(4,128)} %successor.3, f32[4096,128]{1,0:T(8,128)} %get-tuple-element.22.w.weight, ...), custom_call_target="tpu_custom_call" | custom-call | tf_op jit(solution)/shard_map/third/pallas_call | solution.py:335
  357.1 3.5 all-to-all-start.3
  360.6 1.3 slice_reduce_fusion
  362.0 8.7 %all-to-all-done.3 = f32[16,32,128]{2,1,0:T(8,128)S(1)} async-done(((f32[16,32,128]{2,1,0:T(8,128)}), f32[16,32,128]{2,1,0:T(8,128)S(1)}, u32[]{:S(2)}, u32[]{:S(2)}) %all-to-all-start.3) | async-done | bytes 262176 | tf_op jit(solution)/shard_map/all_to_all | solution.py:318
  370.6 0.0 copy-start.1
  370.6 0.7 copy-done.1
  371.4 34.9 %last.1 = f32[16,8192]{1,0:T(8,128)} custom-call(f32[8192,128]{1,0:T(8,128)} %get-tuple-element.20.own, f32[512,128]{1,0:T(8,128)} %bitcast.7, f32[8192,128]{1,0:T(8,128)} %get-tuple-element.30.landed_in, s32[1,16,256]{2,1,0:T(8,128)} %send_rows.7), custom_call_target="tpu_custom_call" | custom-call | tf_op jit(solution)/shard_map/last/pallas_call | solution.py:339
  (1 shorter events, 0.0 us)
Async XLA Ops:
  17.9 17.4 %all-to-all-start = ((f32[16,32,128]{2,1,0:T(8,128)}), f32[16,32,128]{2,1,0:T(8,128)S(1)}, u32[]{:S(2)}, u32[]{:S(2)}) async-start(f32[16,32,128]{2,1,0:T(8,128)} %bitcast.8), calls=%async_computation | async-start | bytes 524288 | tf_op jit(solution)/shard_map/all_to_all | solution.py:318
  35.3 0.7 copy-start
  357.1 13.5 %all-to-all-start.3 = ((f32[16,32,128]{2,1,0:T(8,128)}), f32[16,32,128]{2,1,0:T(8,128)S(1)}, u32[]{:S(2)}, u32[]{:S(2)}) async-start(f32[16,32,128]{2,1,0:T(8,128)} %get-tuple-element.29), calls=%async_computation.3 | async-start | bytes 524288 | tf_op jit(solution)/shard_map/all_to_all | solution.py:318
  370.6 0.7 copy-start.1

commit v2 on v1

--- a/solution.py
+++ b/solution.py
@@ -33,19 +33,19 @@
     return pl.ds(pl.multiple_of(start, size), size)
 
 
-def pack_send(table, send_rows, out, dests):
-    _, peers, slots = send_rows.shape
+def pack_send(table, send_rows, out, dests, peers):
+    slots = send_rows.shape[0] // peers
     groups = LANES // dests
     per = slots // groups
     where = group_of(1, dests)
 
     @pl.loop(0, peers)
     def _(i):
-        @pl.loop(0, per, unroll=4)
+        @pl.loop(0, per, unroll=8)
         def _(r):
-            row = table[pl.ds(send_rows[0, i, r], 1), :]
+            row = table[pl.ds(send_rows[i * slots + r], 1), :]
             for c in range(1, groups):
-                other = table[pl.ds(send_rows[0, i, c * per + r], 1), :]
+                other = table[pl.ds(send_rows[i * slots + c * per + r], 1), :]
                 row = jnp.where(where == c, other, row)
             out[pl.ds(i * per + r, 1), :] = row
 
@@ -69,22 +69,22 @@
 
 
 def gather(table, successor, out, dests):
-    edges, seg = successor.shape
-    half = seg // 2
+    half = out.shape[0]
+    edges = LANES // (2 * dests)
     where = group_of(1, dests)
 
-    @pl.loop(0, half, unroll=4)
+    @pl.loop(0, half, unroll=8)
     def _(r):
         row = None
         for c in range(2 * edges):
-            other = table[pl.ds(successor[c % edges, r + (c // edges) * half], 1), :]
+            other = table[pl.ds(successor[(c % edges * 2 + c // edges) * half + r], 1), :]
             row = other if row is None else jnp.where(where == c, other, row)
         out[pl.ds(r, 1), :] = row
 
 
 def scatter(tables, flow, successor, dests):
-    edges, seg = successor.shape
-    half = seg // 2
+    half = flow.shape[0]
+    edges = LANES // (2 * dests)
     step = half // len(tables)
     where = group_of(1, dests)
 
@@ -100,26 +100,26 @@
             r = r0 + n * step
             row = flow[pl.ds(r, 1), :]
             for c in range(2 * edges):
-                at = table.at[pl.ds(successor[c % edges, r + (c // edges) * half], 1), :]
+                at = table.at[pl.ds(successor[(c % edges * 2 + c // edges) * half + r], 1), :]
                 work.append((at, at[...] + row, where == c))
         for at, value, mask in work:
             pltpu.store(at, value, mask=mask)
 
 
-def settle(table, received, send_rows, dests):
-    _, peers, slots = send_rows.shape
+def settle(table, received, send_rows, dests, peers):
+    slots = send_rows.shape[0] // peers
     groups = LANES // dests
     per = slots // groups
     where = group_of(1, dests)
 
     @pl.loop(0, peers)
     def _(i):
-        @pl.loop(0, per, unroll=2)
+        @pl.loop(0, per, unroll=4)
         def _(r):
             row = received[pl.ds(i * per + r, 1), :]
             work = []
             for c in range(groups):
-                at = table.at[pl.ds(send_rows[0, i, c * per + r], 1), :]
+                at = table.at[pl.ds(send_rows[i * slots + c * per + r], 1), :]
                 work.append((at, at[...] + row, where == c))
             for at, value, mask in work:
                 pltpu.store(at, value, mask=mask)
@@ -150,19 +150,19 @@
         send_out[i, pl.ds(0, per), :] = block
 
 
-def start_kernel(value, send_rows, table, send):
+def start_kernel(peers, value, send_rows, table, send):
     dests, seg = value.shape
 
     @pl.loop(0, seg // LANES, unroll=2)
     def _(b):
         table[ds(b * LANES, LANES), :] = rows_of(jnp.exp(value[:, ds(b * LANES, LANES)]))
 
-    pack_send(table, send_rows, send, dests)
-
-
-def first_kernel(own, received, successor, rewards, dest_at, send_rows, new, weight, send, table, got):
-    edges, seg = successor.shape
-    _, peers, slots = send_rows.shape
+    pack_send(table, send_rows, send, dests, peers)
+
+
+def first_kernel(peers, own, received, successor, rewards, dest_at, send_rows, new, weight, send, table, got):
+    edges, seg = rewards.shape
+    slots = send_rows.shape[0] // peers
     half = seg // 2
     dests = LANES // (2 * edges)
     fill(table, own, received, peers, slots, dests)
@@ -184,14 +184,14 @@
             is_dest = line + (h * half + b * LANES) == dest_at[...]
             new[ds(h * half + b * LANES, LANES), :] = jnp.where(is_dest, 1.0, x)
 
-    pack_send(new, send_rows, send, dests)
-
-
-def second_kernel(own, received, successor, weight, dest_at, start_mass, peers, slots,
+    pack_send(new, send_rows, send, dests, peers)
+
+
+def second_kernel(peers, own, received, successor, weight, dest_at, start_mass,
                   values, p_out, inverse, landed, send, table, flow, *more):
-    edges, seg = successor.shape
+    dests, seg = start_mass.shape
     half = seg // 2
-    dests = LANES // (2 * edges)
+    slots = (table.shape[0] - seg) // peers
     fill(table, own, received, peers, slots, dests)
     gather(table, successor, p_out, dests)
     lane = lax.broadcasted_iota(jnp.int32, (LANES, LANES), 1)
@@ -229,10 +229,10 @@
         send[i, pl.ds(per, dests), :] = weighted
 
 
-def third_kernel(own, received, successor, weight, start_mass, p_in, inverse, landed_in, send_rows,
+def third_kernel(peers, own, received, successor, weight, start_mass, p_in, inverse, landed_in, send_rows,
                  edge_visits, landed, send, total_out, table, flow, inward, *more):
-    edges, seg = successor.shape
-    _, peers, slots = send_rows.shape
+    edges, seg = edge_visits.shape
+    slots = send_rows.shape[0] // peers
     half = seg // 2
     dests = LANES // (2 * edges)
     per = slots * dests // LANES
@@ -248,7 +248,7 @@
     def _(b):
         table[ds(b * 64, 64), :] = landed_in[ds(b * 64, 64), :]
 
-    settle(table, inward, send_rows, dests)
+    settle(table, inward, send_rows, dests, peers)
 
     @pl.loop(0, half // LANES)
     def _(b):
@@ -274,14 +274,14 @@
     finish_spread(tables, seg, peers, slots, landed, send, dests)
 
 
-def last_kernel(own, received, landed_in, send_rows, arrival, table):
+def last_kernel(peers, own, received, landed_in, send_rows, arrival, table):
     dests, seg = arrival.shape
 
     @pl.loop(0, seg // 64)
     def _(b):
         table[ds(b * 64, 64), :] = landed_in[ds(b * 64, 64), :]
 
-    settle(table, received, send_rows, dests)
+    settle(table, received, send_rows, dests, peers)
 
     @pl.loop(0, seg // LANES)
     def _(b):
@@ -289,9 +289,9 @@
         arrival[:, at] = (own[at, :] * fold(table[at, :], dests)).T[:dests, :]
 
 
-def call(kernel, specs, shapes, scratch, name):
+def call(kernel, peers, specs, shapes, scratch, name):
     return pl.pallas_call(
-        kernel,
+        functools.partial(kernel, peers),
         in_specs=specs,
         out_specs=[VMEM] * len(shapes),
         out_shape=[jax.ShapeDtypeStruct(s, jnp.float32) for s in shapes],
@@ -313,6 +313,7 @@
     rows, packed, sent = (seg, LANES), (half, LANES), (peers * per, LANES)
     big = (all_rows, LANES)
     more = [big] * (TABLES - 1)
+    successor, send_rows = successor.reshape(-1), send_rows.reshape(-1)
 
     def exchange(x):
         y = lax.all_to_all(
@@ -320,23 +321,20 @@
         )
         return y.reshape(x.shape)
 
-    zero, send = call(start_kernel, [VMEM, SMEM], [rows, sent], [], "start")(value_init, send_rows)
+    zero, send = call(start_kernel, peers, [VMEM, SMEM], [rows, sent], [], "start")(value_init, send_rows)
     one, weight, send = call(
-        first_kernel, [VMEM, VMEM, SMEM, VMEM, VMEM, SMEM], [rows, packed, sent], [big, packed], "first"
+        first_kernel, peers, [VMEM, VMEM, SMEM, VMEM, VMEM, SMEM], [rows, packed, sent], [big, packed], "first"
     )(zero, exchange(send), successor, rewards, dest_at, send_rows)
 
-    def second(own, received, succ, w, d, mass, *rest):
-        second_kernel(own, received, succ, w, d, mass, peers, slots, *rest)
-
     values, p, inverse, landed, send = call(
-        second, [VMEM, VMEM, SMEM, VMEM, VMEM, VMEM],
+        second_kernel, peers, [VMEM, VMEM, SMEM, VMEM, VMEM, VMEM],
         [(dests, seg), packed, rows, rows, (peers, per + dests, LANES)], [big, packed] + more, "second",
     )(one, exchange(send), successor, weight, dest_at, start_mass)
     edge_visits, landed, send, totals = call(
-        third_kernel, [VMEM, VMEM, SMEM, VMEM, VMEM, VMEM, VMEM, VMEM, SMEM],
+        third_kernel, peers, [VMEM, VMEM, SMEM, VMEM, VMEM, VMEM, VMEM, VMEM, SMEM],
         [(edges, seg), rows, (peers, per, LANES), (dests, LANES)], [big, packed, sent] + more, "third",
     )(one, exchange(send), successor, weight, start_mass, p, inverse, landed, send_rows)
-    (arrival,) = call(last_kernel, [VMEM, VMEM, VMEM, SMEM], [(dests, seg)], [rows], "last")(
+    (arrival,) = call(last_kernel, peers, [VMEM, VMEM, VMEM, SMEM], [(dests, seg)], [rows], "last")(
         one, exchange(send).reshape(sent), landed, send_rows
     )
     return values, edge_visits, arrival, totals[:, 0]

time: 407 us -> 317 us (0.78)
  Pallas kernels: 343 us -> 251 us
    pallas_call x5, Pallas kernels: 343 us -> 251 us  [the longest x1 91.2 us: local(): call(second_kernel, peers, [VMEM, VMEM, SMEM, VMEM, VMEM, VMEM], [(dests,...]
where the time goes in v2:
time: 317 us; the launch traced here: 316 us
  Pallas kernels  251 us (79%)
  blocking collectives  30.6 us (10%)
  waiting for transfers between devices  15.9 us (5%)
  starting transfers between devices  10.9 us (3%)
  local copies, waits for them, and re-layouts  6.24 us (2%)
    pallas_call x1, Pallas kernels, local(): call(second_kernel, peers, [VMEM, VMEM, SMEM, VMEM, VMEM, VMEM], [(dests,...  91.2 us
    pallas_call x1, Pallas kernels, local(): call(third_kernel, peers, [VMEM, VMEM, SMEM, VMEM, VMEM, VMEM, VMEM, VMEM...  67.1 us
    pallas_call x1, Pallas kernels, local(): call(first_kernel, peers, [VMEM, VMEM, SMEM, VMEM, VMEM, SMEM], [rows, pa...  53.1 us
    all_to_all x2, blocking collectives, exchange(): lax.all_to_all(x.reshape(peers, -1, LANES), 'region', split_axis=0, conca...  30.6 us
    pallas_call x1, Pallas kernels, local(): call(last_kernel, peers, [VMEM, VMEM, VMEM, SMEM], [(dests, seg)], [rows]...  29.1 us
    all_to_all x2, waiting for transfers between devices, exchange(): lax.all_to_all(x.reshape(peers, -1, LANES), 'region', split_axis=0, conca...  15.9 us
    all_to_all x2, starting transfers between devices, exchange(): lax.all_to_all(x.reshape(peers, -1, LANES), 'region', split_axis=0, conca...  10.9 us
    pallas_call x1, Pallas kernels, local(): call(start_kernel, peers, [VMEM, SMEM], [rows, sent], [], 'start')  10.5 us
  transfers between devices with their start and end apart: 2, of which 2 were waited for; matrix products, arithmetic and copies ran while one was open for 1% of the time, Pallas kernels for 0%

profile of v2, /device:TPU:0, one launch (start us, length us, event | category | flops | bytes accessed | tf_op | source)
XLA Modules:
  0.0 316.0 jit_solution(4171978214008433239)
XLA Ops:
  0.6 1.3 copy.10
  2.0 10.5 %start.1 = (f32[8192,128]{1,0:T(8,128)}, f32[512,128]{1,0:T(8,128)}) custom-call(f32[16,8192]{1,0:T(8,128)} %value.1, s32[4096]{0:T(1024)} %bitcast.15), custom_call_target="tpu_custom_call" | custom-call | tf_op jit(solution)/shard_map/start/pallas_call | solution.py:324
  12.5 7.4 %all-to-all-start = ((f32[16,32,128]{2,1,0:T(8,128)}), f32[16,32,128]{2,1,0:T(8,128)S(1)}, u32[]{:S(2)}, u32[]{:S(2)}) async-start(f32[16,32,128]{2,1,0:T(8,128)} %bitcast.19), calls=%async_computation | async-start | bytes 524288 | tf_op jit(solution)/shard_map/all_to_all | solution.py:319
  19.8 0.7 broadcast_subtract_fusion
  20.5 0.6 broadcast_in_dim_tile.3.dest_at
  21.1 1.6 copy.11
  22.7 7.2 %all-to-all-done = f32[16,32,128]{2,1,0:T(8,128)S(1)} async-done(((f32[16,32,128]{2,1,0:T(8,128)}), f32[16,32,128]{2,1,0:T(8,128)S(1)}, u32[]{:S(2)}, u32[]{:S(2)}) %all-to-all-start) | async-done | bytes 262176 | tf_op jit(solution)/shard_map/all_to_all | solution.py:319
  29.9 0.0 copy-start
  29.9 0.7 copy-done
  30.6 53.1 %first.1 = (f32[8192,128]{1,0:T(8,128)}, f32[4096,128]{1,0:T(8,128)}, f32[512,128]{1,0:T(8,128)}) custom-call(f32[8192,128]{1,0:T(8,128)} %get-tuple-element.18.own, f32[512,128]{1,0:T(8,128)} %bitcast.13, s32[32768]{0:T(1024)} %bitcast.9, f32[4,8192]{1,0:T(4,128)} %rewards.1, s32[1,128]{1,0:T(1,128)} %broadcast_in_dim_tile.3.dest_at, s32[4096]{0:T(1024)} %bitcast.16), custom_call_target="tpu_custom_call" | custom-call | tf_op jit(solution)/shard_map/first/pallas_call | solution.py:325
  83.7 14.2 %all_to_all.20 = f32[16,32,128]{2,1,0:T(8,128)} all-to-all(f32[16,32,128]{2,1,0:T(8,128)} %bitcast.20), channel_id=1, replica_groups=mesh['groups'=2,'region'=16] {'region'}, dimensions={0} | all-to-all | bytes 524288 | tf_op jit(solution)/shard_map/all_to_all | solution.py:319
  98.0 91.2 %second.1 = (f32[16,8192]{1,0:T(8,128)}, f32[4096,128]{1,0:T(8,128)}, f32[8192,128]{1,0:T(8,128)}, f32[8192,128]{1,0:T(8,128)}, f32[16,48,128]{2,1,0:T(8,128)}) custom-call(f32[8192,128]{1,0:T(8,128)} %get-tuple-element.20.own, f32[512,128]{1,0:T(8,128)} %bitcast.12, s32[32768]{0:T(1024)} %bitcast.10, f32[4096,128]{1,0:T(8,128)} %get-tuple-element.22.weight, ...), custom_call_target="tpu_custom_call" | custom-call | tf_op jit(solution)/shard_map/second/pallas_call | solution.py:329
  189.2 16.4 %all_to_all.21.received = f32[16,48,128]{2,1,0:T(8,128)} all-to-all(f32[16,48,128]{2,1,0:T(8,128)} %get-tuple-element.24), channel_id=1, replica_groups=mesh['groups'=2,'region'=16] {'region'}, dimensions={0} | all-to-all | bytes 786432 | tf_op jit(solution)/shard_map/all_to_all | solution.py:319
  205.6 67.1 %third.1 = (f32[4,8192]{1,0:T(4,128)}, f32[8192,128]{1,0:T(8,128)}, f32[16,32,128]{2,1,0:T(8,128)}, f32[16,128]{1,0:T(8,128)}) custom-call(f32[8192,128]{1,0:T(8,128)} %get-tuple-element.20.own, f32[16,48,128]{2,1,0:T(8,128)} %all_to_all.21.received, s32[32768]{0:T(1024)} %bitcast.11, f32[4096,128]{1,0:T(8,128)} %get-tuple-element.22.weight, ...), custom_call_target="tpu_custom_call" | custom-call | tf_op jit(solution)/shard_map/third/pallas_call | solution.py:333
  272.7 3.5 %all-to-all-start.3 = ((f32[16,32,128]{2,1,0:T(8,128)}), f32[16,32,128]{2,1,0:T(8,128)S(1)}, u32[]{:S(2)}, u32[]{:S(2)}) async-start(f32[16,32,128]{2,1,0:T(8,128)} %get-tuple-element.29), calls=%async_computation.3 | async-start | bytes 524288 | tf_op jit(solution)/shard_map/all_to_all | solution.py:319
  276.2 1.3 slice_reduce_fusion
  277.6 8.7 %all-to-all-done.3 = f32[16,32,128]{2,1,0:T(8,128)S(1)} async-done(((f32[16,32,128]{2,1,0:T(8,128)}), f32[16,32,128]{2,1,0:T(8,128)S(1)}, u32[]{:S(2)}, u32[]{:S(2)}) %all-to-all-start.3) | async-done | bytes 262176 | tf_op jit(solution)/shard_map/all_to_all | solution.py:319
  286.2 0.0 copy-start.1
  286.2 0.7 copy-done.1
  287.0 29.1 %last.1 = f32[16,8192]{1,0:T(8,128)} custom-call(f32[8192,128]{1,0:T(8,128)} %get-tuple-element.20.own, f32[512,128]{1,0:T(8,128)} %bitcast.14, f32[8192,128]{1,0:T(8,128)} %get-tuple-element.30.landed_in, s32[4096]{0:T(1024)} %bitcast.18), custom_call_target="tpu_custom_call" | custom-call | tf_op jit(solution)/shard_map/last/pallas_call | solution.py:337
  (1 shorter events, 0.0 us)
Async XLA Ops:
  12.5 17.4 %all-to-all-start = ((f32[16,32,128]{2,1,0:T(8,128)}), f32[16,32,128]{2,1,0:T(8,128)S(1)}, u32[]{:S(2)}, u32[]{:S(2)}) async-start(f32[16,32,128]{2,1,0:T(8,128)} %bitcast.19), calls=%async_computation | async-start | bytes 524288 | tf_op jit(solution)/shard_map/all_to_all | solution.py:319
  29.9 0.7 copy-start
  272.7 13.5 %all-to-all-start.3 = ((f32[16,32,128]{2,1,0:T(8,128)}), f32[16,32,128]{2,1,0:T(8,128)S(1)}, u32[]{:S(2)}, u32[]{:S(2)}) async-start(f32[16,32,128]{2,1,0:T(8,128)} %get-tuple-element.29), calls=%async_computation.3 | async-start | bytes 524288 | tf_op jit(solution)/shard_map/all_to_all | solution.py:319
  286.2 0.7 copy-start.1

commit v3 on v2

--- a/solution.py
+++ b/solution.py
@@ -137,7 +137,7 @@
     per = slots // groups
     where = group_of(per, dests)
 
-    @pl.loop(0, seg // 64)
+    @pl.loop(0, seg // 64, unroll=2)
     def _(b):
         own_out[ds(b * 64, 64), :] = total(tables, ds(b * 64, 64))
 
@@ -153,7 +153,7 @@
 def start_kernel(peers, value, send_rows, table, send):
     dests, seg = value.shape
 
-    @pl.loop(0, seg // LANES, unroll=2)
+    @pl.loop(0, seg // LANES, unroll=4)
     def _(b):
         table[ds(b * LANES, LANES), :] = rows_of(jnp.exp(value[:, ds(b * LANES, LANES)]))
 
@@ -170,7 +170,7 @@
     lane = lax.broadcasted_iota(jnp.int32, (LANES, LANES), 1)
     line = lax.broadcasted_iota(jnp.int32, (LANES, LANES), 0)
 
-    @pl.loop(0, half // LANES)
+    @pl.loop(0, half // LANES, unroll=2)
     def _(b):
         at = ds(b * LANES, LANES)
         both = [jnp.exp(rewards[:, ds(h * half + b * LANES, LANES)]) for h in range(2)]
@@ -218,7 +218,7 @@
         flow[at, :] = jnp.where(lane >= LANES // 2, parts[1], parts[0]) * w
         return weighted
 
-    weighted = lax.fori_loop(0, half // LANES, body, jnp.zeros((dests, LANES), jnp.float32))
+    weighted = lax.fori_loop(0, half // LANES, body, jnp.zeros((dests, LANES), jnp.float32), unroll=2)
     tables = (table,) + more
     scatter(tables, flow, successor, dests)
     finish_spread(tables, seg, peers, slots, landed, send, dests)
@@ -244,13 +244,13 @@
         weighted = weighted + received[i, per:, :]
     total_out[...] = jnp.broadcast_to(jnp.sum(weighted, axis=1, keepdims=True), (dests, LANES))
 
-    @pl.loop(0, seg // 64)
+    @pl.loop(0, seg // 64, unroll=2)
     def _(b):
         table[ds(b * 64, 64), :] = landed_in[ds(b * 64, 64), :]
 
     settle(table, inward, send_rows, dests, peers)
 
-    @pl.loop(0, half // LANES)
+    @pl.loop(0, half // LANES, unroll=2)
     def _(b):
         at = ds(b * LANES, LANES)
         visits, parts = [], []
@@ -277,16 +277,45 @@
 def last_kernel(peers, own, received, landed_in, send_rows, arrival, table):
     dests, seg = arrival.shape
 
-    @pl.loop(0, seg // 64)
+    @pl.loop(0, seg // 64, unroll=2)
     def _(b):
         table[ds(b * 64, 64), :] = landed_in[ds(b * 64, 64), :]
 
     settle(table, received, send_rows, dests, peers)
 
-    @pl.loop(0, seg // LANES)
+    @pl.loop(0, seg // LANES, unroll=4)
     def _(b):
         at = ds(b * LANES, LANES)
-        arrival[:, at] = (own[at, :] * fold(table[at, :], dests)).T[:dests, :]
+        parts = (own[at, :] * table[at, :]).T
+        arrival[:, at] = sum(parts[c : c + dests, :] for c in range(0, LANES, dests))
+
+
+def exchange_kernel(peers, block, out, landing, send_sem, recv_sem):
+    me = lax.axis_index("region")
+    others = [lax.rem(me + d, peers) for d in range(1, peers)]
+    barrier = pltpu.get_barrier_semaphore()
+    for other in others:
+        pl.semaphore_signal(
+            barrier, inc=1, device_id={"region": other}, device_id_type=pl.DeviceIdType.MESH
+        )
+    pl.semaphore_wait(barrier, peers - 1)
+    copies = []
+    for d, other in enumerate(others):
+        copy = pltpu.make_async_remote_copy(
+            src_ref=block.at[other],
+            dst_ref=landing.at[me],
+            send_sem=send_sem.at[d],
+            recv_sem=recv_sem.at[d],
+            device_id={"region": other},
+            device_id_type=pl.DeviceIdType.MESH,
+        )
+        copy.start()
+        copies.append(copy)
+    out[me] = block[me]
+    for d, copy in enumerate(copies):
+        copy.wait()
+        source = lax.rem(me + peers - 1 - d, peers)
+        out[source] = landing[source]
 
 
 def call(kernel, peers, specs, shapes, scratch, name):
@@ -315,27 +344,38 @@
     more = [big] * (TABLES - 1)
     successor, send_rows = successor.reshape(-1), send_rows.reshape(-1)
 
-    def exchange(x):
-        y = lax.all_to_all(
-            x.reshape(peers, -1, LANES), "region", split_axis=0, concat_axis=0, tiled=True
-        )
+    def exchange(x, number):
+        blocks = (peers, x.size // (peers * LANES), LANES)
+        y = pl.pallas_call(
+            functools.partial(exchange_kernel, peers),
+            in_specs=[VMEM],
+            out_specs=VMEM,
+            out_shape=jax.ShapeDtypeStruct(blocks, jnp.float32),
+            scratch_shapes=[
+                pltpu.VMEM(blocks, jnp.float32),
+                pltpu.SemaphoreType.DMA((peers,)),
+                pltpu.SemaphoreType.DMA((peers,)),
+            ],
+            compiler_params=pltpu.CompilerParams(collective_id=number, has_side_effects=True),
+            name=f"exchange{number}",
+        )(x.reshape(blocks))
         return y.reshape(x.shape)
 
     zero, send = call(start_kernel, peers, [VMEM, SMEM], [rows, sent], [], "start")(value_init, send_rows)
     one, weight, send = call(
         first_kernel, peers, [VMEM, VMEM, SMEM, VMEM, VMEM, SMEM], [rows, packed, sent], [big, packed], "first"
-    )(zero, exchange(send), successor, rewards, dest_at, send_rows)
+    )(zero, exchange(send, 0), successor, rewards, dest_at, send_rows)
 
     values, p, inverse, landed, send = call(
         second_kernel, peers, [VMEM, VMEM, SMEM, VMEM, VMEM, VMEM],
         [(dests, seg), packed, rows, rows, (peers, per + dests, LANES)], [big, packed] + more, "second",
-    )(one, exchange(send), successor, weight, dest_at, start_mass)
+    )(one, exchange(send, 1), successor, weight, dest_at, start_mass)
     edge_visits, landed, send, totals = call(
         third_kernel, peers, [VMEM, VMEM, SMEM, VMEM, VMEM, VMEM, VMEM, VMEM, SMEM],
         [(edges, seg), rows, (peers, per, LANES), (dests, LANES)], [big, packed, sent] + more, "third",
-    )(one, exchange(send), successor, weight, start_mass, p, inverse, landed, send_rows)
+    )(one, exchange(send, 2), successor, weight, start_mass, p, inverse, landed, send_rows)
     (arrival,) = call(last_kernel, peers, [VMEM, VMEM, VMEM, SMEM], [(dests, seg)], [rows], "last")(
-        one, exchange(send).reshape(sent), landed, send_rows
+        one, exchange(send, 3).reshape(sent), landed, send_rows
     )
     return values, edge_visits, arrival, totals[:, 0]
 

time: 317 us -> 287 us (0.905)
  blocking collectives: 30.6 us -> 0 us
  Pallas kernels: 251 us -> 280 us
  waiting for transfers between devices: 15.9 us -> 0 us
  starting transfers between devices: 10.9 us -> 0 us
    pallas_call x0 -> x4, Pallas kernels: none -> 52.3 us  [exchange(): pl.pallas_call(functools.partial(exchange_kernel, peers), in_specs=[VMEM]...]
    all_to_all x2 -> x0, blocking collectives: 30.6 us -> none  [exchange(): lax.all_to_all(x.reshape(peers, -1, LANES), 'region', split_axis=0, conca...]
    pallas_call x1, Pallas kernels: 29.1 us -> 13.2 us  [local(): call(last_kernel, peers, [VMEM, VMEM, VMEM, SMEM], [(dests, seg)], [rows]...]
    all_to_all x2 -> x0, waiting for transfers between devices: 15.9 us -> none  [exchange(): lax.all_to_all(x.reshape(peers, -1, LANES), 'region', split_axis=0, conca...]
    all_to_all x2 -> x0, starting transfers between devices: 10.9 us -> none  [exchange(): lax.all_to_all(x.reshape(peers, -1, LANES), 'region', split_axis=0, conca...]
    pallas_call x1, Pallas kernels: 53.1 us -> 48.7 us  [local(): call(first_kernel, peers, [VMEM, VMEM, SMEM, VMEM, VMEM, SMEM], [rows, pa...]
  transfers between devices with their start and end apart: 2 -> 0, of which waited for: 2 -> 0; matrix products, arithmetic and copies ran while one was open for 1% -> 0% of each run, Pallas kernels for 0% -> 0%
where the time goes in v3:
time: 287 us
  Pallas kernels  280 us (98%)
  local copies, waits for them, and re-layouts  4.8 us (2%)
    pallas_call x1, Pallas kernels, local(): call(second_kernel, peers, [VMEM, VMEM, SMEM, VMEM, VMEM, VMEM], [(dests,...  91.5 us
    pallas_call x1, Pallas kernels, local(): call(third_kernel, peers, [VMEM, VMEM, SMEM, VMEM, VMEM, VMEM, VMEM, VMEM...  65.5 us
    pallas_call x4, Pallas kernels, exchange(): pl.pallas_call(functools.partial(exchange_kernel, peers), in_specs=[VMEM]...  52.3 us
    pallas_call x1, Pallas kernels, local(): call(first_kernel, peers, [VMEM, VMEM, SMEM, VMEM, VMEM, SMEM], [rows, pa...  48.7 us
    pallas_call x1, Pallas kernels, local(): call(last_kernel, peers, [VMEM, VMEM, VMEM, SMEM], [(dests, seg)], [rows]...  13.2 us
    pallas_call x1, Pallas kernels, local(): call(start_kernel, peers, [VMEM, SMEM], [rows, sent], [], 'start')  9.31 us

profile of v3, /device:TPU:0, one launch (start us, length us, event | category | flops | bytes accessed | tf_op | source)
XLA Modules:
  0.0 286.6 jit_solution(9686564482320261842)
XLA Ops:
  0.6 0.7 broadcast_subtract_fusion
  1.3 0.6 broadcast_in_dim_tile.3.dest_at
  1.9 1.3 copy.10
  3.2 1.6 copy.11
  4.8 9.3 %start.1 = (f32[8192,128]{1,0:T(8,128)}, f32[512,128]{1,0:T(8,128)}) custom-call(f32[16,8192]{1,0:T(8,128)} %value.1, s32[4096]{0:T(1024)} %bitcast.15), custom_call_target="tpu_custom_call" | custom-call | tf_op jit(solution)/shard_map/start/pallas_call | solution.py:364
  14.1 12.8 %exchange0.1 = f32[16,32,128]{2,1,0:T(8,128)} custom-call(f32[16,32,128]{2,1,0:T(8,128)} %bitcast.20), custom_call_target="tpu_custom_call" | custom-call | tf_op jit(solution)/shard_map/exchange0/pallas_call | solution.py:349
  26.9 48.7 %first.1 = (f32[8192,128]{1,0:T(8,128)}, f32[4096,128]{1,0:T(8,128)}, f32[512,128]{1,0:T(8,128)}) custom-call(f32[8192,128]{1,0:T(8,128)} %get-tuple-element.18.own, f32[512,128]{1,0:T(8,128)} %bitcast.13, s32[32768]{0:T(1024)} %bitcast.9, f32[4,8192]{1,0:T(4,128)} %rewards.1, s32[1,128]{1,0:T(1,128)} %broadcast_in_dim_tile.3.dest_at, s32[4096]{0:T(1024)} %bitcast.16), custom_call_target="tpu_custom_call" | custom-call | tf_op jit(solution)/shard_map/first/pallas_call | solution.py:365
  75.6 12.2 %exchange1.1 = f32[16,32,128]{2,1,0:T(8,128)} custom-call(f32[16,32,128]{2,1,0:T(8,128)} %bitcast.19), custom_call_target="tpu_custom_call" | custom-call | tf_op jit(solution)/shard_map/exchange1/pallas_call | solution.py:349
  87.8 91.5 %second.1 = (f32[16,8192]{1,0:T(8,128)}, f32[4096,128]{1,0:T(8,128)}, f32[8192,128]{1,0:T(8,128)}, f32[8192,128]{1,0:T(8,128)}, f32[16,48,128]{2,1,0:T(8,128)}) custom-call(f32[8192,128]{1,0:T(8,128)} %get-tuple-element.20.own, f32[512,128]{1,0:T(8,128)} %bitcast.12, s32[32768]{0:T(1024)} %bitcast.10, f32[4096,128]{1,0:T(8,128)} %get-tuple-element.22.weight, ...), custom_call_target="tpu_custom_call" | custom-call | tf_op jit(solution)/shard_map/second/pallas_call | solution.py:369
  179.3 14.4 %exchange2.1.received = f32[16,48,128]{2,1,0:T(8,128)} custom-call(f32[16,48,128]{2,1,0:T(8,128)} %get-tuple-element.24.block), custom_call_target="tpu_custom_call" | custom-call | tf_op jit(solution)/shard_map/exchange2/pallas_call | solution.py:349
  193.7 65.5 %third.1 = (f32[4,8192]{1,0:T(4,128)}, f32[8192,128]{1,0:T(8,128)}, f32[16,32,128]{2,1,0:T(8,128)}, f32[16,128]{1,0:T(8,128)}) custom-call(f32[8192,128]{1,0:T(8,128)} %get-tuple-element.20.own, f32[16,48,128]{2,1,0:T(8,128)} %exchange2.1.received, s32[32768]{0:T(1024)} %bitcast.11, f32[4096,128]{1,0:T(8,128)} %get-tuple-element.22.weight, ...), custom_call_target="tpu_custom_call" | custom-call | tf_op jit(solution)/shard_map/third/pallas_call | solution.py:373
  259.3 1.3 slice_reduce_fusion
  260.6 12.9 %exchange3.1 = f32[16,32,128]{2,1,0:T(8,128)} custom-call(f32[16,32,128]{2,1,0:T(8,128)} %get-tuple-element.29.block), custom_call_target="tpu_custom_call" | custom-call | tf_op jit(solution)/shard_map/exchange3/pallas_call | solution.py:349
  273.5 13.2 %last.1 = f32[16,8192]{1,0:T(8,128)} custom-call(f32[8192,128]{1,0:T(8,128)} %get-tuple-element.20.own, f32[512,128]{1,0:T(8,128)} %bitcast.14, f32[8192,128]{1,0:T(8,128)} %get-tuple-element.30.landed_in, s32[4096]{0:T(1024)} %bitcast.18), custom_call_target="tpu_custom_call" | custom-call | tf_op jit(solution)/shard_map/last/pallas_call | solution.py:377
  (1 shorter events, 0.0 us)

commit v4 on v3

--- a/solution.py
+++ b/solution.py
@@ -33,39 +33,50 @@
     return pl.ds(pl.multiple_of(start, size), size)
 
 
-def pack_send(table, send_rows, out, dests, peers):
-    slots = send_rows.shape[0] // peers
+def exchange_table(table, send_rows, send, landing, send_sem, recv_sem, dests, ready):
+    peers, per, _ = send.shape
     groups = LANES // dests
-    per = slots // groups
-    where = group_of(1, dests)
-
-    @pl.loop(0, peers)
-    def _(i):
+    slots = groups * per
+    seg = table.shape[0] - peers * slots
+    where, wide = group_of(1, dests), group_of(per, dests)
+    me = lax.axis_index("region")
+
+    def pack(i):
         @pl.loop(0, per, unroll=8)
         def _(r):
             row = table[pl.ds(send_rows[i * slots + r], 1), :]
             for c in range(1, groups):
                 other = table[pl.ds(send_rows[i * slots + c * per + r], 1), :]
                 row = jnp.where(where == c, other, row)
-            out[pl.ds(i * per + r, 1), :] = row
-
-
-def fill(table, own, received, peers, slots, dests):
-    seg = own.shape[0]
-    groups = LANES // dests
-    per = slots // groups
-    where = group_of(per, dests)
-
-    @pl.loop(0, seg // 64, unroll=2)
-    def _(b):
-        table[ds(b * 64, 64), :] = own[ds(b * 64, 64), :]
-
-    @pl.loop(0, peers)
-    def _(i):
-        block = received[ds(i * per, per), :]
+            send[i, pl.ds(r, 1), :] = row
+
+    def unpack(i, block):
         for c in range(groups):
-            one = fold(jnp.where(where == c, block, 0.0), dests)
+            one = fold(jnp.where(wide == c, block, 0.0), dests)
             table[ds(seg + i * slots + c * per, per), :] = one
+
+    copies = []
+    for d in range(1, peers):
+        other = lax.rem(me + d, peers)
+        pack(other)
+        if d == 1:
+            ready()
+        copy = pltpu.make_async_remote_copy(
+            src_ref=send.at[other],
+            dst_ref=landing.at[me],
+            send_sem=send_sem.at[d],
+            recv_sem=recv_sem.at[d],
+            device_id={"region": other},
+            device_id_type=pl.DeviceIdType.MESH,
+        )
+        copy.start()
+        copies.append(copy)
+    pack(me)
+    unpack(me, send[me])
+    for d, copy in enumerate(copies):
+        copy.wait()
+        source = lax.rem(me + peers - 1 - d, peers)
+        unpack(source, landing[source])
 
 
 def gather(table, successor, out, dests):
@@ -73,7 +84,7 @@
     edges = LANES // (2 * dests)
     where = group_of(1, dests)
 
-    @pl.loop(0, half, unroll=8)
+    @pl.loop(0, half, unroll=16)
     def _(r):
         row = None
         for c in range(2 * edges):
@@ -93,7 +104,7 @@
         def _(b):
             table[ds(b * 64, 64), :] = jnp.zeros((64, LANES), jnp.float32)
 
-    @pl.loop(0, step, unroll=2)
+    @pl.loop(0, step, unroll=4)
     def _(r0):
         work = []
         for n, table in enumerate(tables):
@@ -150,23 +161,28 @@
         send_out[i, pl.ds(0, per), :] = block
 
 
-def start_kernel(peers, value, send_rows, table, send):
+def backup_kernel(peers, value, send_rows, successor, rewards, dest_at, start_mass,
+                  one, weight, values, p_out, inverse, flow, weighted_out,
+                  table, send, landing, send_again, landing_again, send_sem, recv_sem, send_sem_again, recv_sem_again):
     dests, seg = value.shape
+    edges = rewards.shape[0]
+    half = seg // 2
+    me = lax.axis_index("region")
+    barrier = pltpu.get_barrier_semaphore()
+    for d in range(1, peers):
+        pl.semaphore_signal(
+            barrier, inc=1, device_id={"region": lax.rem(me + d, peers)}, device_id_type=pl.DeviceIdType.MESH
+        )
 
     @pl.loop(0, seg // LANES, unroll=4)
     def _(b):
         table[ds(b * LANES, LANES), :] = rows_of(jnp.exp(value[:, ds(b * LANES, LANES)]))
 
-    pack_send(table, send_rows, send, dests, peers)
-
-
-def first_kernel(peers, own, received, successor, rewards, dest_at, send_rows, new, weight, send, table, got):
-    edges, seg = rewards.shape
-    slots = send_rows.shape[0] // peers
-    half = seg // 2
-    dests = LANES // (2 * edges)
-    fill(table, own, received, peers, slots, dests)
-    gather(table, successor, got, dests)
+    exchange_table(
+        table, send_rows, send, landing, send_sem, recv_sem, dests,
+        lambda: pl.semaphore_wait(barrier, peers - 1),
+    )
+    gather(table, successor, p_out, dests)
     lane = lax.broadcasted_iota(jnp.int32, (LANES, LANES), 1)
     line = lax.broadcasted_iota(jnp.int32, (LANES, LANES), 0)
 
@@ -177,25 +193,20 @@
         lines = [jnp.broadcast_to(x[e : e + 1, :], (dests, LANES)) for x in both for e in range(edges)]
         w = jnp.concatenate(lines, axis=0).T
         weight[at, :] = w
-        p = got[at, :] * w
+        p = p_out[at, :] * w
         for h in range(2):
+            here = ds(h * half + b * LANES, LANES)
             mine = (lane >= LANES // 2) == (h == 1)
             x = fold(jnp.where(mine, p, 0.0), dests)
             is_dest = line + (h * half + b * LANES) == dest_at[...]
-            new[ds(h * half + b * LANES, LANES), :] = jnp.where(is_dest, 1.0, x)
-
-    pack_send(new, send_rows, send, dests, peers)
-
-
-def second_kernel(peers, own, received, successor, weight, dest_at, start_mass,
-                  values, p_out, inverse, landed, send, table, flow, *more):
-    dests, seg = start_mass.shape
-    half = seg // 2
-    slots = (table.shape[0] - seg) // peers
-    fill(table, own, received, peers, slots, dests)
+            x = jnp.where(is_dest, 1.0, x)
+            table[here, :] = x
+            one[here, :] = x
+
+    exchange_table(
+        table, send_rows, send_again, landing_again, send_sem_again, recv_sem_again, dests, lambda: None
+    )
     gather(table, successor, p_out, dests)
-    lane = lax.broadcasted_iota(jnp.int32, (LANES, LANES), 1)
-    line = lax.broadcasted_iota(jnp.int32, (LANES, LANES), 0)
 
     def body(b, weighted):
         at = ds(b * LANES, LANES)
@@ -218,15 +229,22 @@
         flow[at, :] = jnp.where(lane >= LANES // 2, parts[1], parts[0]) * w
         return weighted
 
-    weighted = lax.fori_loop(0, half // LANES, body, jnp.zeros((dests, LANES), jnp.float32), unroll=2)
-    tables = (table,) + more
+    weighted_out[...] = lax.fori_loop(
+        0, half // LANES, body, jnp.zeros((dests, LANES), jnp.float32), unroll=2
+    )
+
+
+def push_kernel(peers, flow, successor, weighted, landed, send, *tables):
+    dests = weighted.shape[0]
+    seg = landed.shape[0]
+    slots = (tables[0].shape[0] - seg) // peers
+    per = slots * dests // LANES
     scatter(tables, flow, successor, dests)
     finish_spread(tables, seg, peers, slots, landed, send, dests)
-    per = slots * dests // LANES
 
     @pl.loop(0, peers)
     def _(i):
-        send[i, pl.ds(per, dests), :] = weighted
+        send[i, pl.ds(per, dests), :] = weighted[...]
 
 
 def third_kernel(peers, own, received, successor, weight, start_mass, p_in, inverse, landed_in, send_rows,
@@ -361,15 +379,26 @@
         )(x.reshape(blocks))
         return y.reshape(x.shape)
 
-    zero, send = call(start_kernel, peers, [VMEM, SMEM], [rows, sent], [], "start")(value_init, send_rows)
-    one, weight, send = call(
-        first_kernel, peers, [VMEM, VMEM, SMEM, VMEM, VMEM, SMEM], [rows, packed, sent], [big, packed], "first"
-    )(zero, exchange(send, 0), successor, rewards, dest_at, send_rows)
-
-    values, p, inverse, landed, send = call(
-        second_kernel, peers, [VMEM, VMEM, SMEM, VMEM, VMEM, VMEM],
-        [(dests, seg), packed, rows, rows, (peers, per + dests, LANES)], [big, packed] + more, "second",
-    )(one, exchange(send, 1), successor, weight, dest_at, start_mass)
+    blocks = (peers, per, LANES)
+    one, weight, values, p, inverse, flow, weighted = pl.pallas_call(
+        functools.partial(backup_kernel, peers),
+        in_specs=[VMEM, SMEM, SMEM, VMEM, VMEM, VMEM],
+        out_specs=[VMEM] * 7,
+        out_shape=[
+            jax.ShapeDtypeStruct(x, jnp.float32)
+            for x in (rows, packed, (dests, seg), packed, rows, packed, (dests, LANES))
+        ],
+        scratch_shapes=[pltpu.VMEM(big, jnp.float32)]
+        + [pltpu.VMEM(blocks, jnp.float32)] * 4
+        + [pltpu.SemaphoreType.DMA((peers,))] * 4,
+        compiler_params=pltpu.CompilerParams(
+            collective_id=0, has_side_effects=True, vmem_limit_bytes=56 * 1024 * 1024
+        ),
+        name="backup",
+    )(value_init, send_rows, successor, rewards, dest_at, start_mass)
+    landed, send = call(
+        push_kernel, peers, [VMEM, SMEM, VMEM], [rows, (peers, per + dests, LANES)], [big] + more, "push"
+    )(flow, successor, weighted)
     edge_visits, landed, send, totals = call(
         third_kernel, peers, [VMEM, VMEM, SMEM, VMEM, VMEM, VMEM, VMEM, VMEM, SMEM],
         [(edges, seg), rows, (peers, per, LANES), (dests, LANES)], [big, packed, sent] + more, "third",

time: 287 us -> 255 us (0.89)
  Pallas kernels: 280 us -> 247 us
    pallas_call x4 -> x2, Pallas kernels: 52.3 us -> 25.6 us  [exchange(): pl.pallas_call(functools.partial(exchange_kernel, peers), in_specs=[VMEM]...]
    pallas_call x1, Pallas kernels: 65.5 us -> 62 us  [local(): call(third_kernel, peers, [VMEM, VMEM, SMEM, VMEM, VMEM, VMEM, VMEM, VMEM...]
    pallas_call x3 -> x2, Pallas kernels: 150 us -> 147 us  [the longest x1 105 us: local(): pl.pallas_call(functools.partial(backup_kernel, peers), in_specs=[VMEM, S...]
where the time goes in v4:
time: 255 us; the launch traced here: 254 us
  Pallas kernels  247 us (97%)
  local copies, waits for them, and re-layouts  5.61 us (2%)
    pallas_call x1, Pallas kernels, local(): pl.pallas_call(functools.partial(backup_kernel, peers), in_specs=[VMEM, S...  105 us
    pallas_call x1, Pallas kernels, local(): call(third_kernel, peers, [VMEM, VMEM, SMEM, VMEM, VMEM, VMEM, VMEM, VMEM...  62 us
    pallas_call x1, Pallas kernels, local(): call(push_kernel, peers, [VMEM, SMEM, VMEM], [rows, (peers, per + dests,...  41.3 us
    pallas_call x2, Pallas kernels, exchange(): pl.pallas_call(functools.partial(exchange_kernel, peers), in_specs=[VMEM]...  25.6 us
    pallas_call x1, Pallas kernels, local(): call(last_kernel, peers, [VMEM, VMEM, VMEM, SMEM], [(dests, seg)], [rows]...  13.2 us

profile of v4, /device:TPU:0, one launch (start us, length us, event | category | flops | bytes accessed | tf_op | source)
XLA Modules:
  0.0 254.3 jit_solution(14010167225826470657)
XLA Ops:
  0.6 0.7 broadcast_subtract_fusion
  1.3 0.6 broadcast_in_dim_tile.3.dest_at
  1.9 1.3 copy.10
  3.2 1.6 copy.11
  4.8 105.2 %backup.1 = (f32[8192,128]{1,0:T(8,128)}, f32[4096,128]{1,0:T(8,128)}, f32[16,8192]{1,0:T(8,128)}, f32[4096,128]{1,0:T(8,128)}, f32[8192,128]{1,0:T(8,128)}, /*index=5*/f32[4096,128]{1,0:T(8,128)}, f32[16,128]{1,0:T(8,128)}) custom-call(f32[16,8192]{1,0:T(8,128)} %value.1, s32[4096]{0:T(1024)} %bitcast.9, s32[32768]{0:T(1024)} %bitcast.5, ...), custom_call_target="tpu_custom_call" | custom-call | tf_op jit(solution)/shard_map/backup/pallas_call | solution.py:383
  110.0 41.3 %push.1 = (f32[8192,128]{1,0:T(8,128)}, f32[16,48,128]{2,1,0:T(8,128)}) custom-call(f32[4096,128]{1,0:T(8,128)} %get-tuple-element.19.flow, s32[32768]{0:T(1024)} %bitcast.6, f32[16,128]{1,0:T(8,128)} %get-tuple-element.20.weighted), custom_call_target="tpu_custom_call" | custom-call | tf_op jit(solution)/shard_map/push/pallas_call | solution.py:399
  151.3 12.8 %exchange2.1.received = f32[16,48,128]{2,1,0:T(8,128)} custom-call(f32[16,48,128]{2,1,0:T(8,128)} %get-tuple-element.21.block), custom_call_target="tpu_custom_call" | custom-call | tf_op jit(solution)/shard_map/exchange2/pallas_call | solution.py:367
  164.1 62.0 %third.1 = (f32[4,8192]{1,0:T(4,128)}, f32[8192,128]{1,0:T(8,128)}, f32[16,32,128]{2,1,0:T(8,128)}, f32[16,128]{1,0:T(8,128)}) custom-call(f32[8192,128]{1,0:T(8,128)} %get-tuple-element.18.own, f32[16,48,128]{2,1,0:T(8,128)} %exchange2.1.received, s32[32768]{0:T(1024)} %bitcast.7, f32[4096,128]{1,0:T(8,128)} %get-tuple-element.22.weight, ...), custom_call_target="tpu_custom_call" | custom-call | tf_op jit(solution)/shard_map/third/pallas_call | solution.py:402
  226.1 1.3 slice_reduce_fusion
  227.4 12.8 %exchange3.1 = f32[16,32,128]{2,1,0:T(8,128)} custom-call(f32[16,32,128]{2,1,0:T(8,128)} %get-tuple-element.27.block), custom_call_target="tpu_custom_call" | custom-call | tf_op jit(solution)/shard_map/exchange3/pallas_call | solution.py:367
  240.2 0.0 copy-start
  240.3 13.2 %last.1 = f32[16,8192]{1,0:T(8,128)} custom-call(f32[8192,128]{1,0:T(8,128)} %get-tuple-element.18.own, f32[512,128]{1,0:T(8,128)} %bitcast.8, f32[8192,128]{1,0:T(8,128)} %get-tuple-element.28.landed_in, s32[4096]{0:T(1024)} %bitcast.11), custom_call_target="tpu_custom_call" | custom-call | tf_op jit(solution)/shard_map/last/pallas_call | solution.py:406
  253.5 0.0 copy-done
  253.5 0.8 copy.13
  (1 shorter events, 0.0 us)
Async XLA Ops:
  240.2 13.2 %copy-start = (f32[16,8192]{1,0:T(8,128)S(1)}, f32[16,8192]{1,0:T(8,128)}, u32[]{:S(2)}) copy-start(f32[16,8192]{1,0:T(8,128)} %get-tuple-element.34) | copy-start | bytes 1572868

commit v5 on v4

--- a/solution.py
+++ b/solution.py
@@ -162,8 +162,8 @@
 
 
 def backup_kernel(peers, value, send_rows, successor, rewards, dest_at, start_mass,
-                  one, weight, values, p_out, inverse, flow, weighted_out,
-                  table, send, landing, send_again, landing_again, send_sem, recv_sem, send_sem_again, recv_sem_again):
+                  one, share, values, p_out, flow, weighted_out,
+                  table, weight, send, landing, send_again, landing_again, send_sem, recv_sem, send_sem_again, recv_sem_again):
     dests, seg = value.shape
     edges = rewards.shape[0]
     half = seg // 2
@@ -212,8 +212,7 @@
         at = ds(b * LANES, LANES)
         w = weight[at, :]
         p = p_out[at, :] * w
-        p_out[at, :] = p
-        parts = []
+        starts, inverses = [], []
         for h in range(2):
             here = ds(h * half + b * LANES, LANES)
             mine = (lane >= LANES // 2) == (h == 1)
@@ -223,10 +222,12 @@
             values[:, here] = v
             mass = start_mass[:, here]
             weighted = weighted + mass * v
-            inv = jnp.where(is_dest, 0.0, 1.0 / x)
-            inverse[here, :] = inv
-            parts.append(rows_of(mass) * inv)
-        flow[at, :] = jnp.where(lane >= LANES // 2, parts[1], parts[0]) * w
+            inverses.append(jnp.where(is_dest, 0.0, 1.0 / x))
+            starts.append(rows_of(mass))
+        inv = jnp.where(lane >= LANES // 2, inverses[1], inverses[0])
+        p_out[at, :] = p * inv
+        share[at, :] = w * inv
+        flow[at, :] = jnp.where(lane >= LANES // 2, starts[1], starts[0]) * (w * inv)
         return weighted
 
     weighted_out[...] = lax.fori_loop(
@@ -247,12 +248,12 @@
         send[i, pl.ds(per, dests), :] = weighted[...]
 
 
-def third_kernel(peers, own, received, successor, weight, start_mass, p_in, inverse, landed_in, send_rows,
-                 edge_visits, landed, send, total_out, table, flow, inward, *more):
-    edges, seg = edge_visits.shape
+def third_kernel(peers, own, received, successor, share, landed_in, send_rows,
+                 mass_out, landed, send, total_out, table, flow, inward, *more):
+    seg = own.shape[0]
     slots = send_rows.shape[0] // peers
     half = seg // 2
-    dests = LANES // (2 * edges)
+    dests = total_out.shape[0]
     per = slots * dests // LANES
     lane = lax.broadcasted_iota(jnp.int32, (LANES, LANES), 1)
 
@@ -271,44 +272,58 @@
     @pl.loop(0, half // LANES, unroll=2)
     def _(b):
         at = ds(b * LANES, LANES)
-        visits, parts = [], []
+        parts = []
         for h in range(2):
             here = ds(h * half + b * LANES, LANES)
-            mass = own[here, :] * fold(table[here, :], dests)
-            inv = inverse[here, :]
-            parts.append(mass * inv)
-            visits.append((rows_of(start_mass[:, here]) + mass) * inv)
-        flow[at, :] = jnp.where(lane >= LANES // 2, parts[1], parts[0]) * weight[at, :]
-        seen = jnp.where(lane >= LANES // 2, visits[1], visits[0]) * p_in[at, :]
-        seen = seen.T
+            parts.append(own[here, :] * fold(table[here, :], dests))
+        mass = jnp.where(lane >= LANES // 2, parts[1], parts[0])
+        mass_out[at, :] = mass
+        flow[at, :] = mass * share[at, :]
+
+    tables = (table,) + more
+    scatter(tables, flow, successor, dests)
+    finish_spread(tables, seg, peers, slots, landed, send, dests)
+
+
+def last_kernel(peers, own, received, landed_in, send_rows, arrival, table):
+    dests, seg = arrival.shape
+
+    @pl.loop(0, seg // 64, unroll=2)
+    def _(b):
+        table[ds(b * 64, 64), :] = landed_in[ds(b * 64, 64), :]
+
+    settle(table, received, send_rows, dests, peers)
+
+    @pl.loop(0, seg // LANES, unroll=4)
+    def _(b):
+        at = ds(b * LANES, LANES)
+        parts = (own[at, :] * table[at, :]).T
+        arrival[:, at] = sum(parts[c : c + dests, :] for c in range(0, LANES, dests))
+
+
+def visits_part(start_mass, mass, policy, edge_visits):
+    edges, seg = edge_visits.shape
+    dests = start_mass.shape[0]
+    half = seg // 2
+    lane = lax.broadcasted_iota(jnp.int32, (LANES, LANES), 1)
+
+    @pl.loop(0, half // LANES, unroll=2)
+    def _(b):
+        at = ds(b * LANES, LANES)
+        low, high = [rows_of(start_mass[:, ds(h * half + b * LANES, LANES)]) for h in range(2)]
+        seen = ((jnp.where(lane >= LANES // 2, high, low) + mass[at, :]) * policy[at, :]).T
         lines = [jnp.sum(seen[c * dests : (c + 1) * dests, :], axis=0, keepdims=True) for c in range(2 * edges)]
         for h in range(2):
             edge_visits[:, ds(h * half + b * LANES, LANES)] = jnp.concatenate(
                 lines[h * edges : (h + 1) * edges], axis=0
             )
 
-    tables = (table,) + more
-    scatter(tables, flow, successor, dests)
-    finish_spread(tables, seg, peers, slots, landed, send, dests)
-
-
-def last_kernel(peers, own, received, landed_in, send_rows, arrival, table):
-    dests, seg = arrival.shape
-
-    @pl.loop(0, seg // 64, unroll=2)
-    def _(b):
-        table[ds(b * 64, 64), :] = landed_in[ds(b * 64, 64), :]
-
-    settle(table, received, send_rows, dests, peers)
-
-    @pl.loop(0, seg // LANES, unroll=4)
-    def _(b):
-        at = ds(b * LANES, LANES)
-        parts = (own[at, :] * table[at, :]).T
-        arrival[:, at] = sum(parts[c : c + dests, :] for c in range(0, LANES, dests))
-
-
-def exchange_kernel(peers, block, out, landing, send_sem, recv_sem):
+
+def exchange_visits_kernel(peers, block, start_mass, mass, policy, out, edge_visits, *rest):
+    exchange_kernel(peers, block, out, *rest, beside=lambda: visits_part(start_mass, mass, policy, edge_visits))
+
+
+def exchange_kernel(peers, block, out, landing, send_sem, recv_sem, beside=None):
     me = lax.axis_index("region")
     others = [lax.rem(me + d, peers) for d in range(1, peers)]
     barrier = pltpu.get_barrier_semaphore()
@@ -330,6 +345,8 @@
         copy.start()
         copies.append(copy)
     out[me] = block[me]
+    if beside is not None:
+        beside()
     for d, copy in enumerate(copies):
         copy.wait()
         source = lax.rem(me + peers - 1 - d, peers)
@@ -362,33 +379,34 @@
     more = [big] * (TABLES - 1)
     successor, send_rows = successor.reshape(-1), send_rows.reshape(-1)
 
-    def exchange(x, number):
-        blocks = (peers, x.size // (peers * LANES), LANES)
-        y = pl.pallas_call(
-            functools.partial(exchange_kernel, peers),
-            in_specs=[VMEM],
-            out_specs=VMEM,
-            out_shape=jax.ShapeDtypeStruct(blocks, jnp.float32),
+    def exchange(x, number, kernel, *beside, extra=()):
+        outs = [x.shape, *extra]
+        return pl.pallas_call(
+            functools.partial(kernel, peers),
+            in_specs=[VMEM] * (1 + len(beside)),
+            out_specs=[VMEM] * len(outs),
+            out_shape=[jax.ShapeDtypeStruct(o, jnp.float32) for o in outs],
             scratch_shapes=[
-                pltpu.VMEM(blocks, jnp.float32),
+                pltpu.VMEM(x.shape, jnp.float32),
                 pltpu.SemaphoreType.DMA((peers,)),
                 pltpu.SemaphoreType.DMA((peers,)),
             ],
-            compiler_params=pltpu.CompilerParams(collective_id=number, has_side_effects=True),
+            compiler_params=pltpu.CompilerParams(
+                collective_id=number, has_side_effects=True, vmem_limit_bytes=40 * 1024 * 1024
+            ),
             name=f"exchange{number}",
-        )(x.reshape(blocks))
-        return y.reshape(x.shape)
+        )(x, *beside)
 
     blocks = (peers, per, LANES)
-    one, weight, values, p, inverse, flow, weighted = pl.pallas_call(
+    one, share, values, policy, flow, weighted = pl.pallas_call(
         functools.partial(backup_kernel, peers),
         in_specs=[VMEM, SMEM, SMEM, VMEM, VMEM, VMEM],
-        out_specs=[VMEM] * 7,
+        out_specs=[VMEM] * 6,
         out_shape=[
             jax.ShapeDtypeStruct(x, jnp.float32)
-            for x in (rows, packed, (dests, seg), packed, rows, packed, (dests, LANES))
+            for x in (rows, packed, (dests, seg), packed, packed, (dests, LANES))
         ],
-        scratch_shapes=[pltpu.VMEM(big, jnp.float32)]
+        scratch_shapes=[pltpu.VMEM(big, jnp.float32), pltpu.VMEM(packed, jnp.float32)]
         + [pltpu.VMEM(blocks, jnp.float32)] * 4
         + [pltpu.SemaphoreType.DMA((peers,))] * 4,
         compiler_params=pltpu.CompilerParams(
@@ -399,12 +417,16 @@
     landed, send = call(
         push_kernel, peers, [VMEM, SMEM, VMEM], [rows, (peers, per + dests, LANES)], [big] + more, "push"
     )(flow, successor, weighted)
-    edge_visits, landed, send, totals = call(
-        third_kernel, peers, [VMEM, VMEM, SMEM, VMEM, VMEM, VMEM, VMEM, VMEM, SMEM],
-        [(edges, seg), rows, (peers, per, LANES), (dests, LANES)], [big, packed, sent] + more, "third",
-    )(one, exchange(send, 2), successor, weight, start_mass, p, inverse, landed, send_rows)
+    (received,) = exchange(send, 2, exchange_kernel)
+    mass, landed, send, totals = call(
+        third_kernel, peers, [VMEM, VMEM, SMEM, VMEM, VMEM, SMEM],
+        [packed, rows, blocks, (dests, LANES)], [big, packed, sent] + more, "third",
+    )(one, received, successor, share, landed, send_rows)
+    received, edge_visits = exchange(
+        send, 3, exchange_visits_kernel, start_mass, mass, policy, extra=[(edges, seg)]
+    )
     (arrival,) = call(last_kernel, peers, [VMEM, VMEM, VMEM, SMEM], [(dests, seg)], [rows], "last")(
-        one, exchange(send, 3).reshape(sent), landed, send_rows
+        one, received.reshape(sent), landed, send_rows
     )
     return values, edge_visits, arrival, totals[:, 0]
 

time: 255 us -> 248 us (0.973)
  Pallas kernels: 247 us -> 236 us
  local copies, waits for them, and re-layouts: 5.61 us -> 10.5 us
    pallas_call x3, Pallas kernels: 87.6 us -> 77.7 us  [the longest x1 55.5 us: local(): call(third_kernel, peers, [VMEM, VMEM, SMEM, VMEM, VMEM, SMEM], [packed,...]
    unnamed x5 -> x22, local copies, waits for them, and re-layouts: 3.69 us -> 9.32 us
where the time goes in v5:
time: 248 us
  Pallas kernels  236 us (95%)
  local copies, waits for them, and re-layouts  10.5 us (4%)
    pallas_call x1, Pallas kernels, local(): pl.pallas_call(functools.partial(backup_kernel, peers), in_specs=[VMEM, S...  104 us
    pallas_call x1, Pallas kernels, local(): call(third_kernel, peers, [VMEM, VMEM, SMEM, VMEM, VMEM, SMEM], [packed,...  55.5 us
    pallas_call x1, Pallas kernels, local(): call(push_kernel, peers, [VMEM, SMEM, VMEM], [rows, (peers, per + dests,...  41.3 us
    pallas_call x2, Pallas kernels, exchange(): pl.pallas_call(functools.partial(kernel, peers), in_specs=[VMEM] * (1 + l...  22.2 us
    pallas_call x1, Pallas kernels, local(): call(last_kernel, peers, [VMEM, VMEM, VMEM, SMEM], [(dests, seg)], [rows]...  13.2 us
    unnamed x22, local copies, waits for them, and re-layouts  9.32 us

profile of v5, /device:TPU:0, one launch (start us, length us, event | category | flops | bytes accessed | tf_op | source)
XLA Modules:
  0.0 248.0 jit_solution(16319816898385806012)
XLA Ops:
  0.6 0.7 broadcast_subtract_fusion
  1.3 0.6 broadcast_in_dim_tile.3.dest_at
  1.9 1.3 copy.10
  3.2 1.6 copy.11
  4.8 103.9 %backup.1 = (f32[8192,128]{1,0:T(8,128)}, f32[4096,128]{1,0:T(8,128)}, f32[16,8192]{1,0:T(8,128)}, f32[4096,128]{1,0:T(8,128)}, f32[4096,128]{1,0:T(8,128)}, /*index=5*/f32[16,128]{1,0:T(8,128)}) custom-call(f32[16,8192]{1,0:T(8,128)} %value.1, s32[4096]{0:T(1024)} %bitcast.9, s32[32768]{0:T(1024)} %bitcast.6, f32[4,8192]{1,0:T(4,128)} %rewards.1, ...), custom_call_target="tpu_custom_call" | custom-call | tf_op jit(solution)/shard_map/backup/pallas_call | solution.py:401
  108.7 41.3 %push.1 = (f32[8192,128]{1,0:T(8,128)}, f32[16,48,128]{2,1,0:T(8,128)}) custom-call(f32[4096,128]{1,0:T(8,128)} %get-tuple-element.20.flow, s32[32768]{0:T(1024)} %bitcast.7, f32[16,128]{1,0:T(8,128)} %get-tuple-element.21.weighted), custom_call_target="tpu_custom_call" | custom-call | tf_op jit(solution)/shard_map/push/pallas_call | solution.py:417
  150.0 0.0 copy-start.4
  150.0 1.0 copy-done.4
  150.9 11.0 %exchange2.1.received = f32[16,48,128]{2,1,0:T(8,128)S(1)} custom-call(f32[16,48,128]{2,1,0:T(8,128)S(1)} %copy-done.4), custom_call_target="tpu_custom_call" | custom-call | tf_op jit(solution)/shard_map/exchange2/pallas_call | solution.py:384
  162.0 0.0 copy-start.3
  162.0 0.7 copy-done.3
  162.7 0.0 copy-start
  162.7 0.0 copy-start.1
  162.7 55.5 %third.1 = (f32[4096,128]{1,0:T(8,128)}, f32[8192,128]{1,0:T(8,128)}, f32[16,32,128]{2,1,0:T(8,128)}, f32[16,128]{1,0:T(8,128)}) custom-call(f32[8192,128]{1,0:T(8,128)} %get-tuple-element.19.own, f32[16,48,128]{2,1,0:T(8,128)} %copy-done.3, s32[32768]{0:T(1024)} %bitcast.8, f32[4096,128]{1,0:T(8,128)} %get-tuple-element.23.share, ...), custom_call_target="tpu_custom_call" | custom-call | tf_op jit(solution)/shard_map/third/pallas_call | solution.py:421
  218.2 0.0 copy-done
  218.2 0.0 copy-done.1
  218.3 0.0 copy-start.2
  218.3 1.6 copy-done.2
  219.8 0.0 copy-start.5
  219.8 0.9 copy-done.5
  220.8 11.2 %exchange3.1 = (f32[16,32,128]{2,1,0:T(8,128)S(1)}, f32[4,8192]{1,0:T(4,128)S(1)}) custom-call(f32[16,32,128]{2,1,0:T(8,128)S(1)} %copy-done.5, f32[16,8192]{1,0:T(8,128)S(1)} %copy-done, f32[4096,128]{1,0:T(8,128)S(1)} %copy-done.2, f32[4096,128]{1,0:T(8,128)S(1)} %copy-done.1), custom_call_target="tpu_custom_call" | custom-call | tf_op jit(solution)/shard_map/exchange3/pallas_call | solution.py:384
  232.0 0.0 copy-start.6
  232.0 0.7 copy-done.6
  232.7 0.0 copy-start.8
  232.7 0.0 copy-start.7
  232.7 13.2 %last.1 = f32[16,8192]{1,0:T(8,128)} custom-call(f32[8192,128]{1,0:T(8,128)} %get-tuple-element.19.own, f32[512,128]{1,0:T(8,128)} %bitcast.5, f32[8192,128]{1,0:T(8,128)} %get-tuple-element.30.landed_in, s32[4096]{0:T(1024)} %bitcast.11), custom_call_target="tpu_custom_call" | custom-call | tf_op jit(solution)/shard_map/last/pallas_call | solution.py:428
  245.9 0.0 copy-done.8
  245.9 0.6 slice_reduce_fusion
  246.6 0.0 copy-done.7
  246.6 0.8 copy.14
  247.3 0.7 copy.15
  (1 shorter events, 0.0 us)
Async XLA Ops:
  150.0 1.0 copy-start.4
  162.0 0.7 copy-start.3
  162.7 55.5 %copy-start = (f32[16,8192]{1,0:T(8,128)S(1)}, f32[16,8192]{1,0:T(8,128)}, u32[]{:S(2)}) copy-start(f32[16,8192]{1,0:T(8,128)} %start_mass.3) | copy-start | bytes 1572868
  162.7 55.5 %copy-start.1 = (f32[4096,128]{1,0:T(8,128)S(1)}, f32[4096,128]{1,0:T(8,128)}, u32[]{:S(2)}) copy-start(f32[4096,128]{1,0:T(8,128)} %get-tuple-element.27.policy) | copy-start | bytes 6291460
  218.3 1.6 copy-start.2
  219.8 0.9 copy-start.5
  232.0 0.7 copy-start.6
  232.7 13.2 %copy-start.8 = (f32[16,128]{1,0:T(8,128)S(1)}, f32[16,128]{1,0:T(8,128)}, u32[]{:S(2)}) copy-start(f32[16,128]{1,0:T(8,128)} %get-tuple-element.31) | copy-start | bytes 24580
  232.7 13.8 %copy-start.7 = (f32[16,8192]{1,0:T(8,128)S(1)}, f32[16,8192]{1,0:T(8,128)}, u32[]{:S(2)}) copy-start(f32[16,8192]{1,0:T(8,128)} %get-tuple-element.36) | copy-start | bytes 1572868
